TPU v7x, 256 devices: a whole 4x4x8 slice. The times are simulated.
256 devices in a mesh: lat: 64 (over z, y, x_hi), wid: 4 (over x_lo, core).
Axes of the slice: x: 4 (x_hi: 2, x_lo: 2; x = x_hi * 2 + x_lo), y: 4, z: 8, core: 2. Of those that a mesh axis runs over, the one named last changes fastest.
Arguments:
- tokens: bfloat16 [2, 256, 3584], P(None, None, 'wid'), may hold values from -6 to 6
- encoder: bfloat16 [3584, 65536], P('wid', 'lat'), may hold values from -0.09375 to 0.09375
- decoder: bfloat16 [65536, 3584], P('lat', 'wid'), may hold values from -0.09375 to 0.09375
- enc_bias: float32 [65536], P('lat'), may hold values from -3 to 3
- dec_bias: float32 [3584], P('wid'), may hold values from -3 to 3
- packed_masks: int32 [2, 16, 65536], P(None, None, 'lat'), may hold values from 0 to 65535
Outputs:
- grad_encoder: float32 [3584, 65536], P('wid', 'lat')
- grad_decoder: float32 [65536, 3584], P('lat', 'wid')
- grad_enc_bias: float32 [65536], P('lat')
- grad_dec_bias: float32 [3584], P('wid')
All inputs are finite; a program needn't handle non-finite values.
Results may differ from a plain program's by a relative error of at most 0.022.
Values may be sent and summed in bfloat16 or wider, within the bound.
No kernel may reach another device: no remote copies, remote signals or barrier semaphores. Data moves between devices by JAX's collectives and lax.ppermute only.
A program may use at most 64 MiB of HBM per device.

v0:
```python
import jax
import jax.numpy as jnp
from jax import lax
from jax.sharding import PartitionSpec as P

MB_TOK = 256


def unpack_bits(words):
    shifts = jnp.arange(16, dtype=jnp.int32)
    bits = jnp.bitwise_and(jnp.right_shift(words[:, None, :], shifts[None, :, None]), 1)
    return bits.reshape(-1, words.shape[-1]).astype(jnp.float32)


def one_pass(inputs_now, gating, encoder, decoder, enc_bias, dec_bias):
    partial_value = jnp.dot(inputs_now, encoder, preferred_element_type=jnp.float32)
    preact = (
        lax.psum(partial_value.astype(jnp.bfloat16), "wid").astype(jnp.float32) + enc_bias[None, :]
    )
    activity = (preact * gating).astype(jnp.bfloat16)
    partial_recon = jnp.dot(activity, decoder, preferred_element_type=jnp.float32)
    summed = lax.psum(partial_recon, "lat")
    residue = summed + dec_bias[None, :] - inputs_now.astype(jnp.float32)
    scaled_error = (residue / MB_TOK).astype(jnp.bfloat16)
    partial_grad = lax.dot_general(
        scaled_error, decoder, (((1,), (1,)), ((), ())), preferred_element_type=jnp.float32
    )
    latent_grad = lax.psum(partial_grad.astype(jnp.bfloat16), "wid").astype(jnp.float32)
    pre_grad = latent_grad * gating
    grad_enc = lax.dot_general(
        inputs_now,
        pre_grad.astype(jnp.bfloat16),
        (((0,), (0,)), ((), ())),
        preferred_element_type=jnp.float32,
    )
    grad_dec = lax.dot_general(
        activity, scaled_error, (((0,), (0,)), ((), ())), preferred_element_type=jnp.float32
    )
    return (grad_enc, grad_dec, jnp.sum(pre_grad, axis=0), jnp.sum(residue, axis=0) / MB_TOK)


def shards(tokens, encoder, decoder, enc_bias, dec_bias, packed_masks):
    micro_count = tokens.shape[0]
    grad_encoder = jnp.zeros(encoder.shape, jnp.float32)
    grad_decoder = jnp.zeros(decoder.shape, jnp.float32)
    grad_enc_bias = jnp.zeros(enc_bias.shape, jnp.float32)
    grad_dec_bias = jnp.zeros(dec_bias.shape, jnp.float32)
    for micro in range(micro_count):
        gating = unpack_bits(packed_masks[micro])
        step_enc, step_dec, step_benc, step_bdec = one_pass(
            tokens[micro], gating, encoder, decoder, enc_bias, dec_bias
        )
        grad_encoder = grad_encoder + step_enc
        grad_decoder = grad_decoder + step_dec
        grad_enc_bias = grad_enc_bias + step_benc
        grad_dec_bias = grad_dec_bias + step_bdec
    return (grad_encoder, grad_decoder, grad_enc_bias, grad_dec_bias)


def solution(mesh):
    in_specs = (
        P(None, None, "wid"),
        P("wid", "lat"),
        P("lat", "wid"),
        P("lat"),
        P("wid"),
        P(None, None, "lat"),
    )
    out_specs = (P("wid", "lat"), P("lat", "wid"), P("lat"), P("wid"))
    return jax.shard_map(shards, mesh=mesh, in_specs=in_specs, out_specs=out_specs, check_vma=False)
```

profile of v0, /device:TPU:1, one launch (start us, length us, event | category | flops | bytes accessed | tf_op | source)
XLA Modules:
  0.0 824.9 jit_solution(6023295225422046046)
XLA Ops:
  7.2 0.0 all-reduce.11.cloned.1.call-start
  7.2 3.3 convolution_convert_fusion.3
  10.6 1.5 convolution_convert_fusion.1
  12.1 0.0 all-reduce.7.cloned.1.call-start
  12.2 0.1 shift_right_arithmetic.48
  12.3 50.9 %all-reduce.11.cloned.1.call-done = (bf16[256,1024]{1,0:T(8,128)(2,1)}, bf16[256,1024]{1,0:T(8,128)(2,1)}) async-done(((bf16[256,1024]{1,0:T(8,128)(2,1)}, bf16[256,1024]{1,0:T(8,128)(2,1)}), (bf16[256,1024]{1,0:T(8,128)(2,1)}, bf16[256,1024]{1,0:T(8,128)(2,1)})) %all-reduce.11.cloned.1.call-update) | async-done | bytes 1048592 | tf_op jit(solution)/shard_map/psum | solution.py:18
  63.1 1.7 fusion.4
  64.8 1.6 fusion.25
  66.5 1.6 fusion.26
  68.1 0.0 all-reduce.9.cloned.1.call-start
  68.2 650.2 %all-reduce.7.cloned.1.call-done = (f32[256,896]{1,0:T(8,128)}, f32[256,896]{1,0:T(8,128)}) async-done(((f32[256,896]{1,0:T(8,128)}, f32[256,896]{1,0:T(8,128)}), (f32[256,896]{1,0:T(8,128)}, f32[256,896]{1,0:T(8,128)})) %all-reduce.7.cloned.1.call-update) | async-done | bytes 1835024 | tf_op jit(solution)/shard_map/psum | solution.py:22
  718.4 2.1 fusion.15
  720.5 1.5 convolution_convert_fusion.2
  722.0 1.6 convolution_convert_fusion
  723.6 0.6 add_multiply_fusion
  724.2 0.7 fusion.27
  725.0 0.3 copy-done.4
  725.2 2.6 convolution_add_fusion
  727.8 79.9 %all-reduce.9.cloned.1.call-done = (bf16[256,1024]{1,0:T(8,128)(2,1)}, bf16[256,1024]{1,0:T(8,128)(2,1)}) async-done(((bf16[256,1024]{1,0:T(8,128)(2,1)}, bf16[256,1024]{1,0:T(8,128)(2,1)}), (bf16[256,1024]{1,0:T(8,128)(2,1)}, bf16[256,1024]{1,0:T(8,128)(2,1)})) %all-reduce.9.cloned.1.call-update) | async-done | bytes 1048592 | tf_op jit(solution)/shard_map/psum | solution.py:28
  807.8 1.7 fusion.10
  809.5 0.8 fusion.18
  810.3 2.5 add_bitcast_fusion
  812.8 5.0 copy.10
  817.8 0.6 add.65
  (22 shorter events, 0.1 us)
Async XLA Ops:
  7.2 57.7 %copy-start = (bf16[1024,896]{1,0:T(8,128)(2,1)S(1)}, bf16[1024,896]{1,0:T(8,128)(2,1)}, u32[]{:S(2)}) copy-start(bf16[1024,896]{1,0:T(8,128)(2,1)} %param.8) | copy-start | bytes 5505028
  7.2 3.4 copy-start.1
  7.2 55.9 %all-reduce.11.cloned.1.call-start = ((), (), s32[]{:S(2)}) async-start(), calls=%async_computation.2 | async-start | bytes 2097152 | tf_op jit(solution)/shard_map/psum | solution.py:18
  7.2 3.3 copy-start.8
  10.5 1.7 copy-start.5
  10.6 52.6 %copy-start.6 = (f32[1024]{0:T(1024)S(1)}, f32[1024]{0:T(1024)}, u32[]{:S(2)}) copy-start(f32[1024]{0:T(1024)} %param.9) | copy-start | bytes 12292
  12.1 706.3 %all-reduce.7.cloned.1.call-start = ((), (), s32[]{:S(2)}) async-start(), calls=%async_computation | async-start | bytes 3670016 | tf_op jit(solution)/shard_map/psum | solution.py:22
  66.5 651.9 %copy-start.7 = (f32[896]{0:T(1024)S(1)}, f32[896]{0:T(1024)}, u32[]{:S(2)}) copy-start(f32[896]{0:T(1024)} %param.10) | copy-start | bytes 10756
  68.1 739.6 %all-reduce.9.cloned.1.call-start = ((), (), s32[]{:S(2)}) async-start(), calls=%async_computation.1 | async-start | bytes 2097152 | tf_op jit(solution)/shard_map/psum | solution.py:28
  720.5 1.5 copy-start.3
  724.2 1.0 copy-start.4
  727.8 81.7 %copy-start.2 = (bf16[2,256,896]{2,1,0:T(8,128)(2,1)S(1)}, bf16[2,256,896]{2,1,0:T(8,128)(2,1)}, u32[]{:S(2)}) copy-start(bf16[2,256,896]{2,1,0:T(8,128)(2,1)} %param.6) | copy-start | bytes 2752516
Sparse Core Ops, SparseCore 0:
  12.2 50.8 all-reduce.10
  68.3 650.0 all-reduce.6
  723.7 83.9 all-reduce.8
where the time goes:
time: 825 us
  waiting for transfers between devices  781 us (95%)
  matrix products  17.8 us (2%)
  between operations  13.8 us (2%)
    psum x1, waiting for transfers between devices, one_pass(): summed = lax.psum(partial_recon, 'lat')  650 us
    psum x1, waiting for transfers between devices, one_pass(): lax.psum(partial_grad.astype(jnp.bfloat16), 'wid').astype(jnp.float32)  79.9 us
    psum x1, waiting for transfers between devices, one_pass(): lax.psum(partial_value.astype(jnp.bfloat16), 'wid').astype(jnp.float32)  50.9 us
  transfers between devices with their start and end apart: 3, of which 3 were waited for; matrix products, arithmetic and copies ran while one was open for 0% of the time, Pallas kernels for 0%

commit v1 on v0

v1 whole, which is shorter than its diff:
```python
import jax
import jax.numpy as jnp
from jax import lax
from jax.sharding import Mesh
from jax.sharding import PartitionSpec as P

MB_TOK = 256
HALF = 128
LAT = ("z", "y", "xh")
WID = ("xl", "c")
N_LAT = 64
ROWS = MB_TOK // N_LAT
SWAP = [(0, 1), (1, 0)]
f32, bf16 = jnp.float32, jnp.bfloat16


def unpack_bits(words):
    shifts = jnp.arange(16, dtype=jnp.int32)
    bits = jnp.bitwise_and(jnp.right_shift(words[:, None, :], shifts[None, :, None]), 1)
    return bits.reshape(-1, words.shape[-1])


def own_first(halves, c):
    own = lax.dynamic_index_in_dim(halves, c, 0, keepdims=False)
    other = lax.dynamic_index_in_dim(halves, 1 - c, 0, keepdims=False)
    return own, other


def wid_sum(part):
    got = lax.ppermute(part[HALF:], "c", SWAP)
    chip = (part[:HALF].astype(f32) + got.astype(f32)).astype(bf16)
    away = lax.ppermute(chip, "xl", SWAP)
    return chip.astype(f32) + away.astype(f32)


def shards(tokens, encoder, decoder, enc_bias, dec_bias, masks):
    c = lax.axis_index("c")
    lat = lax.axis_index(LAT)
    micros = tokens.shape[0]
    toks, gates, acts, errs, pres = [], [], [], [], []
    for m in range(micros):
        own, other = own_first(tokens[m].reshape(2, HALF, -1), c)
        toks.append(jnp.concatenate([own, other], axis=0))
        words = lax.dynamic_slice_in_dim(masks[m], c * 8, 8, axis=0)
        gates.append(unpack_bits(words))
    for m in range(micros):
        part = jnp.dot(toks[m], encoder, preferred_element_type=f32).astype(bf16)
        preact = wid_sum(part) + enc_bias[None, :]
        own = jnp.where(gates[m] != 0, preact, 0.0).astype(bf16)
        other = lax.ppermute(own, "c", SWAP)
        acts.append(jnp.concatenate([own, other], axis=0))
    for m in range(micros):
        recon = jnp.dot(acts[m], decoder, preferred_element_type=f32).astype(bf16)
        pieces = lax.all_to_all(recon.reshape(N_LAT, ROWS, -1), LAT, 0, 0)
        summed = jnp.sum(pieces.astype(f32), axis=0)
        mine = lax.dynamic_slice_in_dim(toks[m], lat * ROWS, ROWS, axis=0)
        residue = summed + dec_bias[None, :] - mine.astype(f32)
        err = (residue / MB_TOK).astype(bf16)
        errs.append(lax.all_to_all(jnp.broadcast_to(err[None], (N_LAT,) + err.shape), LAT, 0, 0).reshape(MB_TOK, -1))
    for m in range(micros):
        part = lax.dot_general(errs[m], decoder, (((1,), (1,)), ((), ())), preferred_element_type=f32).astype(bf16)
        pre_grad = jnp.where(gates[m] != 0, wid_sum(part), 0.0).astype(bf16)
        other = lax.ppermute(pre_grad, "c", SWAP)
        pres.append(jnp.concatenate([pre_grad, other], axis=0))
    tok = jnp.concatenate(toks, axis=0)
    act = jnp.concatenate(acts, axis=0)
    err = jnp.concatenate(errs, axis=0)
    pre = jnp.concatenate(pres, axis=0)
    rows = (((0,), (0,)), ((), ()))
    grad_enc = lax.dot_general(tok, pre, rows, preferred_element_type=f32)
    grad_dec = lax.dot_general(act, err, rows, preferred_element_type=f32)
    return grad_enc, grad_dec, jnp.sum(pre.astype(f32), axis=0), jnp.sum(err.astype(f32), axis=0)


def solution(mesh):
    fine = Mesh(mesh.devices.reshape(8, 4, 2, 2, 2), LAT + WID)
    in_specs = (P(None, None, WID), P(WID, LAT), P(LAT, WID), P(LAT), P(WID), P(None, None, LAT))
    out_specs = (P(WID, LAT), P(LAT, WID), P(LAT), P(WID))
    return jax.shard_map(shards, mesh=fine, in_specs=in_specs, out_specs=out_specs, check_vma=False)
```

time: 825 us -> 154 us (0.19)
  waiting for transfers between devices: 781 us -> 59.1 us
  starting transfers between devices: 0.12 us -> 45.4 us
  blocking collectives: 0 us -> 20.4 us
  between operations: 13.8 us -> 1.02 us
    psum x3 -> x0, waiting for transfers between devices: 781 us -> none  [the longest x1 650 us: one_pass(): summed = lax.psum(partial_recon, 'lat')]
    all_to_all x0 -> x3, waiting for transfers between devices: none -> 34 us  [the longest x2 25.5 us: shards(): pieces = lax.all_to_all(recon.reshape(N_LAT, ROWS, -1), LAT, 0, 0)]
    all_to_all x0 -> x3, starting transfers between devices: none -> 27.2 us  [the longest x2 19.5 us: shards(): pieces = lax.all_to_all(recon.reshape(N_LAT, ROWS, -1), LAT, 0, 0)]
    ppermute x0 -> x12, waiting for transfers between devices: none -> 25.1 us  [the longest x4 22.3 us: wid_sum(): away = lax.ppermute(chip, 'xl', SWAP)]
    all_to_all x0 -> x1, blocking collectives: none -> 20.4 us  [shards(): lax.all_to_all(jnp.broadcast_to(err[None], (N_LAT,) + err.shape), LAT, 0, 0)]
    ppermute x0 -> x12, starting transfers between devices: none -> 18.2 us  [the longest x4 12.1 us: wid_sum(): got = lax.ppermute(part[HALF:], 'c', SWAP)]
    dot_general x10 -> x8, matrix products: 17.8 us -> 11.4 us  [the longest x1 3.15 us: shards(): grad_dec = lax.dot_general(act, err, rows, preferred_element_type=f32)]
  transfers between devices with their start and end apart: 3 -> 15, of which waited for: 3 -> 10; matrix products, arithmetic and copies ran while one was open for 0% -> 9% of each run, Pallas kernels for 0% -> 0%
where the time goes in v1:
time: 154 us; the launch traced here: 153 us
  waiting for transfers between devices  59.1 us (38%)
  starting transfers between devices  45.4 us (29%)
  blocking collectives  20.4 us (13%)
  matrix products  11.4 us (7%)
  local copies, waits for them, and re-layouts  10.1 us (7%)
  other arithmetic  5.58 us (4%)
    all_to_all x2, waiting for transfers between devices, shards(): pieces = lax.all_to_all(recon.reshape(N_LAT, ROWS, -1), LAT, 0, 0)  25.5 us
    ppermute x4, waiting for transfers between devices, wid_sum(): away = lax.ppermute(chip, 'xl', SWAP)  22.3 us
    all_to_all x1, blocking collectives, shards(): lax.all_to_all(jnp.broadcast_to(err[None], (N_LAT,) + err.shape), LAT, 0, 0)  20.4 us
    all_to_all x2, starting transfers between devices, shards(): pieces = lax.all_to_all(recon.reshape(N_LAT, ROWS, -1), LAT, 0, 0)  19.5 us
    ppermute x4, starting transfers between devices, wid_sum(): got = lax.ppermute(part[HALF:], 'c', SWAP)  12.1 us
    all_to_all x1, waiting for transfers between devices, shards(): lax.all_to_all(jnp.broadcast_to(err[None], (N_LAT,) + err.shape), LAT, 0, 0)  8.53 us
    all_to_all x1, starting transfers between devices, shards(): lax.all_to_all(jnp.broadcast_to(err[None], (N_LAT,) + err.shape), LAT, 0, 0)  7.64 us
    unnamed x45, local copies, waits for them, and re-layouts  3.24 us
  transfers between devices with their start and end apart: 15, of which 10 were waited for; matrix products, arithmetic and copies ran while one was open for 9% of the time, Pallas kernels for 0%

profile of v1, /device:TPU:1, one launch (start us, length us, event | category | flops | bytes accessed | tf_op | source)
XLA Modules:
  0.0 153.0 jit_solution(4984040454477346846)
XLA Ops:
  0.7 1.4 fusion.34
  2.2 1.6 %copy-done.17 = bf16[896,1024]{1,0:T(8,128)(2,1)S(1)} copy-done((bf16[896,1024]{1,0:T(8,128)(2,1)S(1)}, bf16[896,1024]{1,0:T(8,128)(2,1)}, u32[]{:S(2)}) %copy-start.17) | copy-done | bytes 1835032
  5.3 3.2 %collective-permute-start.6 = (bf16[128,1024]{1,0:T(8,128)(2,1)}, bf16[128,1024]{1,0:T(8,128)(2,1)}, u32[]{:S(2)}, u32[]{:S(2)}) collective-permute-start(bf16[128,1024]{1,0:T(8,128)(2,1)} %slice.53), channel_id=1, source_target_pairs={{0,1},{1,0},{2,3},{3,2},{4,5},{5,4},{6,7},{7,6},{8,9},{9,8},{10,11... | collective-permute-start | bytes 786440 | tf_op jit(solution)/shard_map/ppermute | solution.py:30
  10.1 1.1 add_convert_fusion.1
  12.9 5.7 %collective-permute-done.7 = bf16[128,1024]{1,0:T(8,128)(2,1)S(1)} collective-permute-done((bf16[128,1024]{1,0:T(8,128)(2,1)S(1)}, bf16[128,1024]{1,0:T(8,128)(2,1)S(1)}, u32[]{:S(2)}, u32[]{:S(2)}) %collective-permute-start.7) | collective-permute-done | bytes 262176 | tf_op jit(solution)/shard_map/ppermute | solution.py:32
  18.6 5.6 %collective-permute-done.1 = bf16[128,1024]{1,0:T(8,128)(2,1)S(1)} collective-permute-done((bf16[128,1024]{1,0:T(8,128)(2,1)S(1)}, bf16[128,1024]{1,0:T(8,128)(2,1)S(1)}, u32[]{:S(2)}, u32[]{:S(2)}) %collective-permute-start.1) | collective-permute-done | bytes 262176 | tf_op jit(solution)/shard_map/ppermute | solution.py:32
  24.6 1.4 collective-permute-start.8
  26.0 1.2 collective-permute-done.8
  29.5 12.5 %all-to-all-start.2 = ((bf16[64,4,896]{2,1,0:T(4,128)(2,1)}), bf16[64,4,896]{2,1,0:T(4,128)(2,1)S(1)}, u32[]{:S(2)}, u32[]{:S(2)}) async-start(bf16[64,4,896]{2,1,0:T(4,128)(2,1)} %reshape.38), calls=%async_computation.2 | async-start | bytes 917504 | tf_op jit(solution)/shard_map/all_to_all | solution.py:54
  42.8 1.2 collective-permute-done.2
  44.7 1.7 %convolution_convert_fusion.5 = bf16[256,896]{1,0:T(8,128)(2,1)S(1)} fusion(bf16[1024,896]{1,0:T(8,128)(2,1)S(1)} %copy-done, bf16[128,1024]{1,0:T(8,128)(2,1)S(1)} %collective-permute-done.2, bf16[128,1024]{1,0:T(8,128)(2,1)} %copy-done.10), kind=kOutput, calls=%fused_computation.7 | convolution fusion | flops 471040000 | bytes 2818048 | tf_op jit(solution)/shard_map/dot_general | solution.py:53
  47.2 10.9 %all-to-all-done.2 = bf16[64,4,896]{2,1,0:T(4,128)(2,1)S(1)} async-done(((bf16[64,4,896]{2,1,0:T(4,128)(2,1)}), bf16[64,4,896]{2,1,0:T(4,128)(2,1)S(1)}, u32[]{:S(2)}, u32[]{:S(2)}) %all-to-all-start.2) | async-done | bytes 458784 | tf_op jit(solution)/shard_map/all_to_all | solution.py:54
  58.1 7.0 %all-to-all-start = ((bf16[64,4,896]{2,1,0:T(4,128)(2,1)}), bf16[64,4,896]{2,1,0:T(4,128)(2,1)S(1)}, u32[]{:S(2)}, u32[]{:S(2)}) async-start(bf16[64,4,896]{2,1,0:T(4,128)(2,1)} %reshape.36), calls=%async_computation | async-start | bytes 917504 | tf_op jit(solution)/shard_map/all_to_all | solution.py:54
  65.4 14.5 %all-to-all-done = bf16[64,4,896]{2,1,0:T(4,128)(2,1)S(1)} async-done(((bf16[64,4,896]{2,1,0:T(4,128)(2,1)}), bf16[64,4,896]{2,1,0:T(4,128)(2,1)S(1)}, u32[]{:S(2)}, u32[]{:S(2)}) %all-to-all-start) | async-done | bytes 458784 | tf_op jit(solution)/shard_map/all_to_all | solution.py:54
  81.0 20.4 %all_to_all.20 = bf16[64,4,896]{2,1,0:T(4,128)(2,1)S(1)} all-to-all(bf16[64,4,896]{2,1,0:T(4,128)(2,1)S(1)} %broadcast_in_dim.13), channel_id=1, replica_groups=mesh['z'=8,'y'=4,'xh'=2,'xl'=2,'c'=2] {'z','y','xh'}, dimensions={0} | all-to-all | bytes 917504 | tf_op jit(solution)/shard_map/all_to_all | solution.py:59
  102.3 7.6 %all-to-all-start.1 = ((bf16[64,4,896]{2,1,0:T(4,128)(2,1)}), bf16[64,4,896]{2,1,0:T(4,128)(2,1)S(1)}, u32[]{:S(2)}, u32[]{:S(2)}) async-start(bf16[64,4,896]{2,1,0:T(4,128)(2,1)} %broadcast_in_dim.12), calls=%async_computation.1 | async-start | bytes 917504 | tf_op jit(solution)/shard_map/all_to_all | solution.py:59
  111.7 3.3 %collective-permute-start.9 = (bf16[128,1024]{1,0:T(8,128)(2,1)}, bf16[128,1024]{1,0:T(8,128)(2,1)}, u32[]{:S(2)}, u32[]{:S(2)}) collective-permute-start(bf16[128,1024]{1,0:T(8,128)(2,1)} %slice.55), channel_id=1, source_target_pairs={{0,1},{1,0},{2,3},{3,2},{4,5},{5,4},{6,7},{7,6},{8,9},{9,8},{10,11... | collective-permute-start | bytes 786440 | tf_op jit(solution)/shard_map/ppermute | solution.py:30
  115.0 8.5 %all-to-all-done.1 = bf16[64,4,896]{2,1,0:T(4,128)(2,1)S(1)} async-done(((bf16[64,4,896]{2,1,0:T(4,128)(2,1)}), bf16[64,4,896]{2,1,0:T(4,128)(2,1)S(1)}, u32[]{:S(2)}, u32[]{:S(2)}) %all-to-all-start.1) | async-done | bytes 458784 | tf_op jit(solution)/shard_map/all_to_all | solution.py:59
  124.4 5.6 %collective-permute-start.3 = (bf16[128,1024]{1,0:T(8,128)(2,1)S(1)}, bf16[128,1024]{1,0:T(8,128)(2,1)S(1)}, u32[]{:S(2)}, u32[]{:S(2)}) collective-permute-start(bf16[128,1024]{1,0:T(8,128)(2,1)S(1)} %slice.51), channel_id=1, source_target_pairs={{0,1},{1,0},{2,3},{3,2},{4,5},{5,4},{6,7},{7,6},{8,9},{9,8},{10,11... | collective-permute-start | bytes 786440 | tf_op jit(solution)/shard_map/ppermute | solution.py:30
  131.6 1.2 collective-permute-start.4
  133.7 5.4 %collective-permute-done.10 = bf16[128,1024]{1,0:T(8,128)(2,1)S(1)} collective-permute-done((bf16[128,1024]{1,0:T(8,128)(2,1)S(1)}, bf16[128,1024]{1,0:T(8,128)(2,1)S(1)}, u32[]{:S(2)}, u32[]{:S(2)}) %collective-permute-start.10) | collective-permute-done | bytes 262176 | tf_op jit(solution)/shard_map/ppermute | solution.py:32
  139.0 5.6 %collective-permute-done.4 = bf16[128,1024]{1,0:T(8,128)(2,1)S(1)} collective-permute-done((bf16[128,1024]{1,0:T(8,128)(2,1)S(1)}, bf16[128,1024]{1,0:T(8,128)(2,1)S(1)}, u32[]{:S(2)}, u32[]{:S(2)}) %collective-permute-start.4) | collective-permute-done | bytes 262176 | tf_op jit(solution)/shard_map/ppermute | solution.py:32
  146.1 3.1 %fusion = f32[1024,896]{1,0:T(8,128)} fusion(bf16[512,896]{1,0:T(8,128)(2,1)S(1)} %constant_dynamic-update-slice_fusion, bf16[128,1024]{1,0:T(8,128)(2,1)S(1)} %copy-done.19, bf16[128,1024]{1,0:T(8,128)(2,1)S(1)} %copy-done.13, bf16[128,1024]{1,0:T(8,128)(2,1)S(1)} %copy-done.21, bf16[128,1024]{1,0:T(8,128)(2,1)S(1)} %copy-done.11), kind=kOutput, calls=%fused_computation.9 | convolution fusion | flops 943718400 | bytes 5636096 | tf_op jit(solution)/shard_map/dot_general | solution.py:71
  150.0 3.0 %fusion.8 = f32[896,1024]{1,0:T(8,128)} fusion(bf16[128,896]{1,0:T(8,128)(2,1)S(1)} %copy-done.2, bf16[128,896]{1,0:T(8,128)(2,1)S(1)} %get-tuple-element.8, bf16[128,896]{1,0:T(8,128)(2,1)S(1)} %copy-done.4, bf16[128,896]{1,0:T(8,128)(2,1)S(1)} %copy-done.6, bf16[128,1024]{1,0:T(8,128)(2,1)S(1)} %collective-permute-done.11, ...), kind=kOutput, calls=%fused_computation.17 | convolution fusion | flops 947388416 | bytes 5636096 | tf_op jit(solution)/shard_map/dot_general | solution.py:70
  (88 shorter events, 19.1 us)
Async XLA Ops:
  0.6 27.3 %copy-start = (bf16[1024,896]{1,0:T(8,128)(2,1)S(1)}, bf16[1024,896]{1,0:T(8,128)(2,1)}, u32[]{:S(2)}) copy-start(bf16[1024,896]{1,0:T(8,128)(2,1)} %param.8) | copy-start | bytes 5505028
  2.1 78.0 %copy-start.1 = (bf16[128,896]{1,0:T(8,128)(2,1)}, bf16[128,896]{1,0:T(8,128)(2,1)S(1)}, u32[]{:S(2)}) copy-start(bf16[128,896]{1,0:T(8,128)(2,1)S(1)} %get-tuple-element.9) | copy-start | bytes 688132
  2.1 78.0 %copy-start.3 = (bf16[128,896]{1,0:T(8,128)(2,1)}, bf16[128,896]{1,0:T(8,128)(2,1)S(1)}, u32[]{:S(2)}) copy-start(bf16[128,896]{1,0:T(8,128)(2,1)S(1)} %get-tuple-element.18) | copy-start | bytes 688132
  5.3 4.8 %collective-permute-start.6 = (bf16[128,1024]{1,0:T(8,128)(2,1)}, bf16[128,1024]{1,0:T(8,128)(2,1)}, u32[]{:S(2)}, u32[]{:S(2)}) collective-permute-start(bf16[128,1024]{1,0:T(8,128)(2,1)} %slice.53), channel_id=1, source_target_pairs={{0,1},{1,0},{2,3},{3,2},{4,5},{5,4},{6,7},{7,6},{8,9},{9,8},{10,11... | collective-permute-start | bytes 786440 | tf_op jit(solution)/shard_map/ppermute | solution.py:30
  9.3 15.0 %copy-start.15 = (f32[1024]{0:T(1024)S(1)}, f32[1024]{0:T(1024)}, u32[]{:S(2)}) copy-start(f32[1024]{0:T(1024)} %param.9) | copy-start | bytes 12292
  10.0 1.7 %collective-permute-start = (bf16[128,1024]{1,0:T(8,128)(2,1)}, bf16[128,1024]{1,0:T(8,128)(2,1)S(1)}, u32[]{:S(2)}, u32[]{:S(2)}) collective-permute-start(bf16[128,1024]{1,0:T(8,128)(2,1)} %slice.49), channel_id=1, source_target_pairs={{0,1},{1,0},{2,3},{3,2},{4,5},{5,4},{6,7},{7,6},{8,9},{9,8},{10,11... | collective-permute-start | bytes 786440 | tf_op jit(solution)/shard_map/ppermute | solution.py:30
  11.2 7.4 %collective-permute-start.7 = (bf16[128,1024]{1,0:T(8,128)(2,1)S(1)}, bf16[128,1024]{1,0:T(8,128)(2,1)S(1)}, u32[]{:S(2)}, u32[]{:S(2)}) collective-permute-start(bf16[128,1024]{1,0:T(8,128)(2,1)S(1)} %add_convert_fusion.1), channel_id=1, source_target_pairs={{0,2},{2,0},{1,3},{3,1},{4,6},{6,4},{5,7},{7,5},{8,10},{10,8},{9,1... | collective-permute-start | bytes 786440 | tf_op jit(solution)/shard_map/ppermute | solution.py:32
  11.8 12.4 %collective-permute-start.1 = (bf16[128,1024]{1,0:T(8,128)(2,1)S(1)}, bf16[128,1024]{1,0:T(8,128)(2,1)S(1)}, u32[]{:S(2)}, u32[]{:S(2)}) collective-permute-start(bf16[128,1024]{1,0:T(8,128)(2,1)S(1)} %add_convert_fusion.3), channel_id=1, source_target_pairs={{0,2},{2,0},{1,3},{3,1},{4,6},{6,4},{5,7},{7,5},{8,10},{10,8},{9,1... | collective-permute-start | bytes 786440 | tf_op jit(solution)/shard_map/ppermute | solution.py:32
  24.6 17.5 %copy-start.10 = (bf16[128,1024]{1,0:T(8,128)(2,1)}, bf16[128,1024]{1,0:T(8,128)(2,1)S(1)}, u32[]{:S(2)}) copy-start(bf16[128,1024]{1,0:T(8,128)(2,1)S(1)} %get-tuple-element.12) | copy-start | bytes 786436
  24.6 2.6 %collective-permute-start.8 = (bf16[128,1024]{1,0:T(8,128)(2,1)S(1)}, bf16[128,1024]{1,0:T(8,128)(2,1)S(1)}, u32[]{:S(2)}, u32[]{:S(2)}) collective-permute-start(bf16[128,1024]{1,0:T(8,128)(2,1)S(1)} %get-tuple-element.13), channel_id=1, source_target_pairs={{0,1},{1,0},{2,3},{3,2},{4,5},{5,4},{6,7},{7,6},{8,9},{9,8},{10,11... | collective-permute-start | bytes 786440 | tf_op jit(solution)/shard_map/ppermute | solution.py:50
  29.5 28.6 %all-to-all-start.2 = ((bf16[64,4,896]{2,1,0:T(4,128)(2,1)}), bf16[64,4,896]{2,1,0:T(4,128)(2,1)S(1)}, u32[]{:S(2)}, u32[]{:S(2)}) async-start(bf16[64,4,896]{2,1,0:T(4,128)(2,1)} %reshape.38), calls=%async_computation.2 | async-start | bytes 917504 | tf_op jit(solution)/shard_map/all_to_all | solution.py:54
  42.1 1.9 %collective-permute-start.2 = (bf16[128,1024]{1,0:T(8,128)(2,1)S(1)}, bf16[128,1024]{1,0:T(8,128)(2,1)S(1)}, u32[]{:S(2)}, u32[]{:S(2)}) collective-permute-start(bf16[128,1024]{1,0:T(8,128)(2,1)S(1)} %get-tuple-element.12), channel_id=1, source_target_pairs={{0,1},{1,0},{2,3},{3,2},{4,5},{5,4},{6,7},{7,6},{8,9},{9,8},{10,11... | collective-permute-start | bytes 786440 | tf_op jit(solution)/shard_map/ppermute | solution.py:50
  46.3 33.8 %copy-start.16 = (f32[896]{0:T(1024)S(1)}, f32[896]{0:T(1024)}, u32[]{:S(2)}) copy-start(f32[896]{0:T(1024)} %param.10) | copy-start | bytes 10756
  58.1 21.8 %all-to-all-start = ((bf16[64,4,896]{2,1,0:T(4,128)(2,1)}), bf16[64,4,896]{2,1,0:T(4,128)(2,1)S(1)}, u32[]{:S(2)}, u32[]{:S(2)}) async-start(bf16[64,4,896]{2,1,0:T(4,128)(2,1)} %reshape.36), calls=%async_computation | async-start | bytes 917504 | tf_op jit(solution)/shard_map/all_to_all | solution.py:54
  102.3 21.2 %all-to-all-start.1 = ((bf16[64,4,896]{2,1,0:T(4,128)(2,1)}), bf16[64,4,896]{2,1,0:T(4,128)(2,1)S(1)}, u32[]{:S(2)}, u32[]{:S(2)}) async-start(bf16[64,4,896]{2,1,0:T(4,128)(2,1)} %broadcast_in_dim.12), calls=%async_computation.1 | async-start | bytes 917504 | tf_op jit(solution)/shard_map/all_to_all | solution.py:59
  111.7 18.3 %collective-permute-start.9 = (bf16[128,1024]{1,0:T(8,128)(2,1)}, bf16[128,1024]{1,0:T(8,128)(2,1)}, u32[]{:S(2)}, u32[]{:S(2)}) collective-permute-start(bf16[128,1024]{1,0:T(8,128)(2,1)} %slice.55), channel_id=1, source_target_pairs={{0,1},{1,0},{2,3},{3,2},{4,5},{5,4},{6,7},{7,6},{8,9},{9,8},{10,11... | collective-permute-start | bytes 786440 | tf_op jit(solution)/shard_map/ppermute | solution.py:30
  124.4 7.1 %collective-permute-start.3 = (bf16[128,1024]{1,0:T(8,128)(2,1)S(1)}, bf16[128,1024]{1,0:T(8,128)(2,1)S(1)}, u32[]{:S(2)}, u32[]{:S(2)}) collective-permute-start(bf16[128,1024]{1,0:T(8,128)(2,1)S(1)} %slice.51), channel_id=1, source_target_pairs={{0,1},{1,0},{2,3},{3,2},{4,5},{5,4},{6,7},{7,6},{8,9},{9,8},{10,11... | collective-permute-start | bytes 786440 | tf_op jit(solution)/shard_map/ppermute | solution.py:30
  131.1 8.0 %collective-permute-start.10 = (bf16[128,1024]{1,0:T(8,128)(2,1)S(1)}, bf16[128,1024]{1,0:T(8,128)(2,1)S(1)}, u32[]{:S(2)}, u32[]{:S(2)}) collective-permute-start(bf16[128,1024]{1,0:T(8,128)(2,1)S(1)} %add_convert_fusion), channel_id=1, source_target_pairs={{0,2},{2,0},{1,3},{3,1},{4,6},{6,4},{5,7},{7,5},{8,10},{10,8},{9,1... | collective-permute-start | bytes 786440 | tf_op jit(solution)/shard_map/ppermute | solution.py:32
  131.6 14.5 %copy-start.11 = (bf16[128,1024]{1,0:T(8,128)(2,1)S(1)}, bf16[128,1024]{1,0:T(8,128)(2,1)}, u32[]{:S(2)}) copy-start(bf16[128,1024]{1,0:T(8,128)(2,1)} %copy-done.10) | copy-start | bytes 786436
  131.6 14.5 %copy-start.13 = (bf16[128,1024]{1,0:T(8,128)(2,1)S(1)}, bf16[128,1024]{1,0:T(8,128)(2,1)}, u32[]{:S(2)}) copy-start(bf16[128,1024]{1,0:T(8,128)(2,1)} %copy-done.12) | copy-start | bytes 786436
  131.6 14.5 %copy-start.19 = (bf16[128,1024]{1,0:T(8,128)(2,1)S(1)}, bf16[128,1024]{1,0:T(8,128)(2,1)}, u32[]{:S(2)}) copy-start(bf16[128,1024]{1,0:T(8,128)(2,1)} %copy-done.18) | copy-start | bytes 786436
  131.6 13.0 %collective-permute-start.4 = (bf16[128,1024]{1,0:T(8,128)(2,1)S(1)}, bf16[128,1024]{1,0:T(8,128)(2,1)S(1)}, u32[]{:S(2)}, u32[]{:S(2)}) collective-permute-start(bf16[128,1024]{1,0:T(8,128)(2,1)S(1)} %add_convert_fusion.2), channel_id=1, source_target_pairs={{0,2},{2,0},{1,3},{3,1},{4,6},{6,4},{5,7},{7,5},{8,10},{10,8},{9,1... | collective-permute-start | bytes 786440 | tf_op jit(solution)/shard_map/ppermute | solution.py:32
  145.0 4.3 %collective-permute-start.5 = (bf16[128,1024]{1,0:T(8,128)(2,1)S(1)}, bf16[128,1024]{1,0:T(8,128)(2,1)S(1)}, u32[]{:S(2)}, u32[]{:S(2)}) collective-permute-start(bf16[128,1024]{1,0:T(8,128)(2,1)S(1)} %get-tuple-element.16), channel_id=1, source_target_pairs={{0,1},{1,0},{2,3},{3,2},{4,5},{5,4},{6,7},{7,6},{8,9},{9,8},{10,11... | collective-permute-start | bytes 786440 | tf_op jit(solution)/shard_map/ppermute | solution.py:63
  145.9 3.3 %collective-permute-start.11 = (bf16[128,1024]{1,0:T(8,128)(2,1)S(1)}, bf16[128,1024]{1,0:T(8,128)(2,1)S(1)}, u32[]{:S(2)}, u32[]{:S(2)}) collective-permute-start(bf16[128,1024]{1,0:T(8,128)(2,1)S(1)} %get-tuple-element.17), channel_id=1, source_target_pairs={{0,1},{1,0},{2,3},{3,2},{4,5},{5,4},{6,7},{7,6},{8,9},{9,8},{10,11... | collective-permute-start | bytes 786440 | tf_op jit(solution)/shard_map/ppermute | solution.py:63
  (13 other events, 54.5 us)

commit v2 on v1

v2 whole, which is shorter than its diff:
```python
import jax
import jax.numpy as jnp
from jax import lax
from jax.experimental import pallas as pl
from jax.experimental.pallas import tpu as pltpu
from jax.sharding import Mesh
from jax.sharding import PartitionSpec as P

MB_TOK = 256
Q = 64
CHUNK = 2 * Q
LAT = ("z", "y", "xh")
WID = ("xl", "c")
FAR = ("z", "xh")
PEERS = 16
ROWS = CHUNK // PEERS
FIRST_LIMIT = 52
FIRST, LAST = (2, 3), (1, 0)
GROUPS = (FIRST, LAST)
ORDER = tuple(r for group in GROUPS for r in group)
SWAP = [(0, 1), (1, 0)]
f32, bf16, i32 = jnp.float32, jnp.bfloat16, jnp.int32
VMEM = pl.BlockSpec(memory_space=pltpu.VMEM)
SMEM = pl.BlockSpec(memory_space=pltpu.SMEM)
ANY = pl.BlockSpec(memory_space=pl.ANY)
TINY = pl.CostEstimate(flops=1, bytes_accessed=1, transcendentals=0)
DOWN = (((0,), (0,)), ((), ()))
ACROSS = (((1,), (1,)), ((), ()))


def call(kernel, outs, args, ids=None, after=(), scratch=(), limit=24):
    skip = len(after)

    def body(*refs):
        kernel(*refs[skip:])

    return pl.pallas_call(
        body,
        out_shape=[jax.ShapeDtypeStruct(s, t) for s, t in outs],
        in_specs=[ANY] * skip + ([] if ids is None else [SMEM]) + [VMEM] * len(args),
        out_specs=[VMEM] * len(outs),
        scratch_shapes=scratch,
        compiler_params=pltpu.CompilerParams(vmem_limit_bytes=limit << 20),
        cost_estimate=TINY,
    )(*after, *([] if ids is None else [ids]), *args)


def encode_first(ids, tokens, encoder, group):
    d, n = encoder.shape
    parts = 4
    rows = len(group) * Q
    order = [2 * r + h for h in (0, 1) for r in group]

    def kernel(ids_ref, tok_hbm, enc_hbm, keep_ref, send_ref, tok, enc, sems):
        pieces = [pl.ds(k * (d // parts), d // parts) for k in range(parts)]
        blocks = [pl.ds(k * (8 // parts), 8 // parts) for k in range(parts)]
        copies = [pltpu.make_async_copy(tok_hbm.at[at], tok.at[at], sems.at[k]) for k, at in enumerate(blocks)]
        copies += [pltpu.make_async_copy(enc_hbm.at[at], enc.at[at], sems.at[parts + k]) for k, at in enumerate(pieces)]
        for copy in copies:
            copy.start()
        for copy in copies:
            copy.wait()
        lhs = jnp.concatenate([tok[ids_ref[at]] for at in order], axis=0)
        for j in range(0, n, 256):
            out = jnp.dot(lhs, enc[:, j:j + 256], preferred_element_type=f32).astype(bf16)
            keep_ref[:, j:j + 256] = out[:rows]
            send_ref[:, j:j + 256] = out[rows:]

    return pl.pallas_call(
        kernel,
        out_shape=[jax.ShapeDtypeStruct(s, bf16) for s in ((rows, n), (rows, n), tokens.shape)],
        in_specs=[SMEM, ANY, ANY],
        out_specs=[VMEM] * 3,
        scratch_shapes=[pltpu.VMEM((d, n), bf16), pltpu.SemaphoreType.DMA((2 * parts,))],
        compiler_params=pltpu.CompilerParams(vmem_limit_bytes=FIRST_LIMIT << 20),
        cost_estimate=TINY,
    )(ids, tokens, encoder)


def encode(ids, tokens, encoder, groups):
    n = encoder.shape[1]
    order = [(2 * r + h, k, h) for k, group in enumerate(groups) for h in (0, 1) for r in group]
    sizes = [len(group) * Q for group in groups for h in (0, 1)]

    def kernel(ids_ref, tok_ref, enc_ref, *outs):
        lhs = jnp.concatenate([tok_ref[ids_ref[at]] for at, _, _ in order], axis=0)
        for j in range(0, n, 256):
            out = jnp.dot(lhs, enc_ref[:, j:j + 256], preferred_element_type=f32).astype(bf16)
            at = 0
            for size, ref in zip(sizes, outs):
                ref[:, j:j + 256] = out[at:at + size]
                at += size

    return call(kernel, [((size, n), bf16) for size in sizes], (tokens, encoder), ids)


def gates(ids, masks, after):
    n = masks.shape[-1]

    def kernel(ids_ref, mask_ref, *outs):
        shift = lax.broadcasted_iota(i32, (16, n), 0)
        for group, out_ref in zip(GROUPS, outs):
            for k, r in enumerate(group):
                words = mask_ref[ids_ref[2 * r]]
                for w in range(Q // 16):
                    bit = jnp.right_shift(jnp.broadcast_to(words[w:w + 1], (16, n)), shift) & 1
                    out_ref[k * Q + 16 * w:k * Q + 16 * w + 16] = bit.astype(f32).astype(bf16)

    return call(kernel, [((len(group) * Q, n), bf16) for group in GROUPS], (masks,), ids, after)


def activity(gate, chip, away, bias, after):
    def kernel(gate_ref, chip_ref, away_ref, bias_ref, out_ref):
        value = chip_ref[...].astype(f32) + away_ref[...].astype(f32) + bias_ref[...].reshape(1, -1)
        out_ref[...] = (value * gate_ref[...].astype(f32)).astype(bf16)

    return call(kernel, [(chip.shape, bf16)], (gate, chip, away, bias), None, after)[0]


def gradient(gate, chip, away, after=()):
    def kernel(gate_ref, chip_ref, away_ref, out_ref):
        value = chip_ref[...].astype(f32) + away_ref[...].astype(f32)
        out_ref[...] = (value * gate_ref[...].astype(f32)).astype(bf16)

    return call(kernel, [(chip.shape, bf16)], (gate, chip, away), None, after)[0]


def decode(own, dec_own, dec_other, after=()):
    n = dec_own.shape[1]
    count = own.shape[0] // Q

    def kernel(own_ref, dec_ref, oth_ref, *outs):
        for k, ref in enumerate((dec_ref, oth_ref)):
            for j in range(0, n, 256):
                at = slice(j, min(j + 256, n))
                out = jnp.dot(own_ref[...], ref[:, at], preferred_element_type=f32).astype(bf16)
                for q, out_ref in enumerate(outs):
                    out_ref[k * Q:k * Q + Q, at] = out[q * Q:q * Q + Q]

    return call(kernel, [((CHUNK, n), bf16)] * count, (own, dec_own, dec_other), None, after)


def bases(ids, tokens, bias):
    shape = ((ROWS, bias.shape[0]), f32)

    def kernel(ids_ref, tok_ref, bias_ref, own_ref, send_ref):
        bias = bias_ref[...].reshape(1, -1)
        own_ref[...] = bias - tok_ref[ids_ref[8]].astype(f32)
        send_ref[...] = bias - tok_ref[ids_ref[9]].astype(f32)

    return call(kernel, [shape, shape], (tokens, bias), ids)


def error(ids, pieces, own, other):
    def kernel(ids_ref, piece_ref, own_ref, other_ref, out_ref):
        total = jnp.where(ids_ref[10] == 0, own_ref[...], other_ref[...])
        for k in range(PEERS):
            total = total + piece_ref[k].astype(f32)
        value = (total / MB_TOK).astype(bf16)
        for k in range(PEERS):
            out_ref[k] = value

    return call(kernel, [(pieces.shape, bf16)], (pieces, own, other), ids)[0]


def back(errs, dec_own, dec_other, after=()):
    n = dec_own.shape[1]
    count = len(errs)

    def kernel(*refs):
        dec_ref, oth_ref, out_ref = refs[count:]
        own = jnp.concatenate([ref[:Q] for ref in refs[:count]], axis=0)
        other = jnp.concatenate([ref[Q:] for ref in refs[:count]], axis=0)
        out = jnp.dot(own, dec_ref[...], preferred_element_type=f32)
        out = out + jnp.dot(other, oth_ref[...], preferred_element_type=f32)
        out_ref[...] = out.astype(bf16)

    return call(kernel, [((count * Q, n), bf16)], (*errs, dec_own, dec_other), None, after)[0]


def flipped(x, after):
    def kernel(x_ref, out_ref, same_ref):
        for j in range(0, x.shape[0], 256):
            block = x_ref[j:j + 256]
            out_ref[:, j:j + 256] = block.T
            same_ref[j:j + 256] = block

    return call(kernel, [(x.shape[::-1], bf16), (x.shape, bf16)], (x,), None, after)


def turned(ids, tokens, after):
    d = tokens.shape[-1]

    def kernel(ids_ref, tok_ref, out_ref):
        at = 0
        for h in (0, 1):
            for group in (ORDER[:2], ORDER[2:]):
                pair = jnp.concatenate([tok_ref[ids_ref[2 * r + h]] for r in group], axis=0)
                out_ref[:, at:at + CHUNK] = pair.T
                at += CHUNK

    return call(kernel, [((d, 4 * CHUNK), bf16)], (tokens,), ids, after)[0]


def decoder_grad(owns, others, errs, err_others, after):
    n, d = others.shape[1], errs[0].shape[1]
    tile = 256
    skip = len(after)
    rows = len(ORDER) * Q

    def kernel(*refs):
        a0, a1, a2, e0, e1, e2, e3, other, out_ref, sum_ref, done_ref, err_ref = refs[skip:]

        @pl.when(pl.program_id(0) == 0)
        def _():
            e = (e0, e1, e2, e3)
            for k, r in enumerate(ORDER):
                err_ref[k * Q:k * Q + Q] = e[r][:Q]
            err_ref[rows:] = other[...]
            sum_ref[...] = jnp.sum(err_ref[...].astype(f32), axis=0)
            done_ref[...] = jnp.zeros_like(done_ref)

        lhs = jnp.concatenate([a0[...], a1[...], a2[...]], axis=0)
        out_ref[...] = lax.dot_general(lhs, err_ref[...], DOWN, preferred_element_type=f32)

    acts = (*owns, others)
    return pl.pallas_call(
        kernel,
        grid=(n // tile,),
        in_specs=[ANY] * skip
        + [pl.BlockSpec((act.shape[0], tile), lambda i: (0, i)) for act in acts]
        + [pl.BlockSpec((CHUNK, d), lambda i: (0, 0))] * 4
        + [pl.BlockSpec((rows, d), lambda i: (0, 0))],
        out_specs=[
            pl.BlockSpec((tile, d), lambda i: (i, 0)),
            pl.BlockSpec((d,), lambda i: (0,)),
            pl.BlockSpec((8, 128), lambda i: (0, 0)),
        ],
        out_shape=[jax.ShapeDtypeStruct((n, d), f32), jax.ShapeDtypeStruct((d,), f32), jax.ShapeDtypeStruct((8, 128), f32)],
        scratch_shapes=[pltpu.VMEM((2 * rows, d), bf16)],
        compiler_params=pltpu.CompilerParams(vmem_limit_bytes=24 << 20),
        cost_estimate=TINY,
    )(*after, *acts, *errs, err_others)


def encoder_grad(tok_t, pres):
    d, n = tok_t.shape[0], pres[0].shape[1]
    parts = 7
    tile = d // parts
    count = len(pres)

    def kernel(t_ref, *refs):
        out_hbm, sum_ref, out, sems = refs[count:]
        pre = jnp.concatenate([ref[...] for ref in refs[:count]], axis=0)
        copies = []
        for k in range(parts):
            rows = pl.ds(k * tile, tile)
            out[rows] = jnp.dot(t_ref[rows], pre, preferred_element_type=f32)
            copies.append(pltpu.make_async_copy(out.at[rows], out_hbm.at[rows], sems.at[k]))
            copies[-1].start()
        sum_ref[...] = jnp.dot(jnp.ones((16, 4 * CHUNK), bf16), pre, preferred_element_type=f32)[0]
        for copy in copies:
            copy.wait()

    return pl.pallas_call(
        kernel,
        in_specs=[VMEM] * (1 + count),
        out_specs=[ANY, VMEM],
        out_shape=[jax.ShapeDtypeStruct((d, n), f32), jax.ShapeDtypeStruct((n,), f32)],
        scratch_shapes=[pltpu.VMEM((d, n), f32), pltpu.SemaphoreType.DMA((parts,))],
        compiler_params=pltpu.CompilerParams(vmem_limit_bytes=24 << 20),
        cost_estimate=TINY,
    )(tok_t, *pres)


def swap(x, axis, name):
    with jax.named_scope(name):
        return lax.ppermute(x, axis, SWAP)


def partner(x, r, name):
    with jax.named_scope(name):
        return lax.ppermute(x, "y", [(i, i ^ r) for i in range(4)])


def add(a, b, after=()):
    def kernel(a_ref, b_ref, out_ref):
        out_ref[...] = (a_ref[...].astype(f32) + b_ref[...].astype(f32)).astype(bf16)

    return call(kernel, [(a.shape, bf16)], (a, b), None, after)[0]


def stacked(parts, after=()):
    rows = [x.shape[0] - at for x, at in parts]

    def kernel(*refs):
        at = 0
        for (_, start), size, ref in zip(parts, rows, refs):
            refs[-1][at:at + size] = ref[start:]
            at += size

    shape = ((sum(rows), parts[0][0].shape[1]), bf16)
    return call(kernel, [shape], [x for x, _ in parts], None, after)[0]


def add3(a, b, c):
    def kernel(a_ref, b_ref, c_ref, out_ref):
        out_ref[...] = a_ref[...].astype(f32) + b_ref[...].astype(f32) + c_ref[...].astype(f32)

    return call(kernel, [(a.shape, f32)], (a, b, c))[0]


def shards(tokens, encoder, decoder, enc_bias, dec_bias, masks):
    c = lax.axis_index("c")
    y = lax.axis_index("y")
    far = lax.axis_index(FAR)
    d = tokens.shape[-1]
    tokens = tokens.reshape(8, Q, d)
    masks = masks.reshape(8, Q // 16, -1)
    groups = Q // ROWS
    k = jnp.arange(11, dtype=i32)
    ids = (y ^ (k >> 1)) * 2 + (c ^ (k & 1))
    ids = jnp.where(k >= 8, (y * 2 + (c ^ (k & 1))) * groups + far % groups, ids)
    ids = jnp.where(k == 10, far // groups, ids)

    keep0, send0, tokens = encode_first(ids, tokens, encoder, FIRST)
    got0 = swap(send0, "c", "got0")
    keep1, send1 = encode(ids, tokens, encoder, (LAST,))
    got1 = swap(send1, "c", "got1")
    chip0 = add(keep0, got0)
    away0 = swap(chip0, "xl", "away0")
    gate0, gate1 = gates(ids, masks, [chip0])
    tok_t = turned(ids, tokens, [chip0])
    chip1 = add(keep1, got1, [tok_t, gate0])
    away1 = swap(chip1, "xl", "away1")
    decoder2 = swap(decoder, "c", "decoder2")
    base, base_send = bases(ids, tokens.reshape(-1, ROWS, d), dec_bias)
    base2 = swap(base_send, "c", "base2")
    dec_t, dec = flipped(decoder, [chip1])
    dec_t2, dec2 = flipped(decoder2, [chip1])
    act0 = activity(gate0, chip0, away0, enc_bias, [dec_t, dec_t2, base2])
    r2, r3 = decode(act0, dec, dec2)
    g2, g3 = partner(r2, 2, "g2"), partner(r3, 3, "g3")
    act1 = activity(gate1, chip1, away1, enc_bias, [r2])
    r1, r0 = decode(act1, dec, dec2)
    g1 = partner(r1, 1, "g1")
    total = add(add3(r0, g2, g3), g1)
    pieces = lax.all_to_all(total.reshape(PEERS, ROWS, d), FAR, 0, 0)
    copies = error(ids, pieces, base, base2)
    e0 = lax.all_to_all(copies, FAR, 0, 0).reshape(CHUNK, d)
    e1, e3, e2 = partner(e0, 1, "e1"), partner(e0, 3, "e3"), partner(e0, 2, "e2")
    part1 = back([e1, e0], dec_t, dec_t2)
    away1 = swap(part1, "xl", "back1")
    part0 = back([e2, e3], dec_t, dec_t2, [part1])
    away0 = swap(part0, "xl", "back0")
    act_others = swap(stacked([(act0, 0), (act1, 0)], [e0]), "c", "act_others")
    err_others = swap(stacked([(e2, Q), (e3, Q), (e1, Q), (e0, Q)]), "c", "err_others")
    pre1 = gradient(gate1, part1, away1, [part0])
    pre1o = swap(pre1, "c", "pre1o")
    grad_dec, dec_sum, done = decoder_grad((act0, act1), act_others, (e0, e1, e2, e3), err_others, [part0])
    pre0 = gradient(gate0, part0, away0, [done, pre1])
    pre0o = swap(pre0, "c", "pre0o")
    grad_enc, enc_sum = encoder_grad(tok_t, [pre0, pre1, pre0o, pre1o])
    return grad_enc, grad_dec, enc_sum, dec_sum


def solution(mesh):
    fine = Mesh(mesh.devices.reshape(8, 4, 2, 2, 2), LAT + WID)
    in_specs = (P(None, None, WID), P(WID, LAT), P(LAT, WID), P(LAT), P(WID), P(None, None, LAT))
    out_specs = (P(WID, LAT), P(LAT, WID), P(LAT), P(WID))
    return jax.shard_map(shards, mesh=fine, in_specs=in_specs, out_specs=out_specs, check_vma=False)
```

time: 154 us -> 100 us (0.65)
  waiting for transfers between devices: 59.1 us -> 20.5 us
  starting transfers between devices: 45.4 us -> 25.4 us
  Pallas kernels: 0 us -> 19.9 us
  blocking collectives: 20.4 us -> 33.2 us
  matrix products: 11.4 us -> 0 us
  local copies, waits for them, and re-layouts: 10.1 us -> 0.07 us
  other arithmetic: 5.58 us -> 0.01 us
    all_to_all x3 -> x0, waiting for transfers between devices: 34 us -> none  [the longest x2 25.5 us: shards(): pieces = lax.all_to_all(recon.reshape(N_LAT, ROWS, -1), LAT, 0, 0)]
    all_to_all x3 -> x0, starting transfers between devices: 27.2 us -> none  [the longest x2 19.5 us: shards(): pieces = lax.all_to_all(recon.reshape(N_LAT, ROWS, -1), LAT, 0, 0)]
    pallas_call x0 -> x24, Pallas kernels: none -> 19.9 us  [the longest x21 10.2 us: call(): pl.pallas_call(body, out_shape=[jax.ShapeDtypeStruct(s, t) for s, t in ou...]
    all_to_all x1 -> x2, blocking collectives: 20.4 us -> 33.2 us  [the longest x1 19.8 us: shards(): pieces = lax.all_to_all(total.reshape(PEERS, ROWS, d), FAR, 0, 0)]
    dot_general x8 -> x0, matrix products: 11.4 us -> none  [the longest x1 3.15 us: shards(): grad_dec = lax.dot_general(act, err, rows, preferred_element_type=f32)]
    ppermute x12 -> x18, starting transfers between devices: 18.2 us -> 25.4 us  [the longest x12 20.2 us: swap(): return lax.ppermute(x, axis, SWAP)]
    ppermute x12 -> x18, waiting for transfers between devices: 25.1 us -> 20.5 us  [the longest x12 11.4 us: swap(): return lax.ppermute(x, axis, SWAP)]
    slice x6 -> x0, local copies, waits for them, and re-layouts: 3.66 us -> none  [the longest x4 2.28 us: wid_sum(): got = lax.ppermute(part[HALF:], 'c', SWAP)]
  transfers between devices with their start and end apart: 15 -> 18, of which waited for: 10 -> 10; matrix products, arithmetic and copies ran while one was open for 9% -> 0% of each run, Pallas kernels for 0% -> 16%
where the time goes in v2:
time: 100 us
  blocking collectives  33.2 us (33%)
  starting transfers between devices  25.4 us (25%)
  waiting for transfers between devices  20.5 us (20%)
  Pallas kernels  19.9 us (20%)
  between operations  1.03 us (1%)
    ppermute x12, starting transfers between devices, swap(): return lax.ppermute(x, axis, SWAP)  20.2 us
    all_to_all x1, blocking collectives, shards(): pieces = lax.all_to_all(total.reshape(PEERS, ROWS, d), FAR, 0, 0)  19.8 us
    all_to_all x1, blocking collectives, shards(): e0 = lax.all_to_all(copies, FAR, 0, 0).reshape(CHUNK, d)  13.4 us
    ppermute x12, waiting for transfers between devices, swap(): return lax.ppermute(x, axis, SWAP)  11.4 us
    pallas_call x21, Pallas kernels, call(): pl.pallas_call(body, out_shape=[jax.ShapeDtypeStruct(s, t) for s, t in ou...  10.2 us
    ppermute x6, waiting for transfers between devices, partner(): return lax.ppermute(x, 'y', [(i, i ^ r) for i in range(4)])  9.19 us
    ppermute x6, starting transfers between devices, partner(): return lax.ppermute(x, 'y', [(i, i ^ r) for i in range(4)])  5.22 us
    pallas_call x1, Pallas kernels, decoder_grad(): pl.pallas_call(kernel, grid=(n // tile,), in_specs=[ANY] * skip + [pl.Blo...  3.67 us
  transfers between devices with their start and end apart: 18, of which 10 were waited for; matrix products, arithmetic and copies ran while one was open for 0% of the time, Pallas kernels for 16%

profile of v2, /device:TPU:1, one launch (start us, length us, event | category | flops | bytes accessed | tf_op | source)
XLA Modules:
  0.0 100.1 jit_solution(17536567529229441986)
XLA Ops:
  0.6 3.3 %collective-permute-start.2 = (bf16[1024,896]{1,0:T(8,128)(2,1)}, bf16[1024,896]{1,0:T(8,128)(2,1)}, u32[]{:S(2)}, u32[]{:S(2)}) collective-permute-start(bf16[1024,896]{1,0:T(8,128)(2,1)} %refs_1_.1), channel_id=1, source_target_pairs={{0,1},{1,0},{2,3},{3,2},{4,5},{5,4},{6,7},{7,6},{8,9},{9,8},{10,11... | collective-permute-start | bytes 5505032 | tf_op jit(solution)/shard_map/decoder2/ppermute | solution.py:278
  4.0 3.2 %shard_map.93 = (bf16[128,1024]{1,0:T(8,128)(2,1)S(1)}, bf16[128,1024]{1,0:T(8,128)(2,1)S(1)}, bf16[8,64,896]{2,1,0:T(8,128)(2,1)S(1)}) custom-call(s32[11]{0:T(128)S(1)} %compare_select_fusion.1.ids_ref.refs_1_.refs_0_, bf16[8,64,896]{2,1,0:T(8,128)(2,1)} %bitcast.13, bf16[896,1024]{1,0:T(8,128)(2,1)} %refs_2_.2), custom_call_target="tpu_custom_call" | custom-call | flops 1 | bytes 1 | tf_op jit(solution)/shard_map/pallas_call | solution.py:69
  7.3 1.2 %shard_map.97 = (bf16[128,1024]{1,0:T(8,128)(2,1)S(1)}, bf16[128,1024]{1,0:T(8,128)(2,1)S(1)}) custom-call(s32[11]{0:T(128)S(1)} %compare_select_fusion.1.ids_ref.refs_1_.refs_0_, bf16[8,64,896]{2,1,0:T(8,128)(2,1)S(1)} %get-tuple-element.28.refs_2_.refs_1_, bf16[896,1024]{1,0:T(8,128)(2,1)S(1)} %copy-done), custom_call_target="tpu_custom_call" | custom-call | flops 1 | bytes 1 | tf_op jit(solution)/shard_map/pallas_call | solution.py:37
  9.3 0.8 shard_map.95.refs_0_.t_ref
  10.9 1.5 %collective-permute-start.5 = (bf16[128,1024]{1,0:T(8,128)(2,1)S(1)}, bf16[128,1024]{1,0:T(8,128)(2,1)S(1)}, u32[]{:S(2)}, u32[]{:S(2)}) collective-permute-start(bf16[128,1024]{1,0:T(8,128)(2,1)S(1)} %shard_map.98.refs_0_.refs_2_), channel_id=1, source_target_pairs={{0,2},{2,0},{1,3},{3,1},{4,6},{6,4},{5,7},{7,5},{8,10},{10,8},{9,1... | collective-permute-start | bytes 786440 | tf_op jit(solution)/shard_map/away1/ppermute | solution.py:278
  14.4 2.1 %shard_map.100 = (bf16[896,1024]{1,0:T(8,128)(2,1)S(1)}, bf16[1024,896]{1,0:T(8,128)(2,1)S(1)}) custom-call(bf16[128,1024]{1,0:T(8,128)(2,1)S(1)} %shard_map.98.refs_0_.refs_2_, bf16[1024,896]{1,0:T(8,128)(2,1)} %collective-permute-done.2.refs_1_), custom_call_target="tpu_custom_call" | custom-call | flops 1 | bytes 1 | tf_op jit(solution)/shard_map/pallas_call | solution.py:37
  17.3 0.7 shard_map.103
  18.0 1.1 %collective-permute-start.7 = (bf16[128,896]{1,0:T(8,128)(2,1)S(1)}, bf16[128,896]{1,0:T(8,128)(2,1)S(1)}, u32[]{:S(2)}, u32[]{:S(2)}) collective-permute-start(bf16[128,896]{1,0:T(8,128)(2,1)S(1)} %get-tuple-element.40), channel_id=1, source_target_pairs={{0,24},{8,16},{16,8},{24,0},{1,25},{9,17},{17,9},{25,1},{2,26},{10... | collective-permute-start | bytes 688136 | tf_op jit(solution)/shard_map/g3/ppermute | solution.py:283
  19.4 3.3 %collective-permute-done.5.refs_3_ = bf16[128,1024]{1,0:T(8,128)(2,1)S(1)} collective-permute-done((bf16[128,1024]{1,0:T(8,128)(2,1)S(1)}, bf16[128,1024]{1,0:T(8,128)(2,1)S(1)}, u32[]{:S(2)}, u32[]{:S(2)}) %collective-permute-start.5) | collective-permute-done | bytes 262176 | tf_op jit(solution)/shard_map/away1/ppermute | solution.py:278
  23.7 6.7 %collective-permute-done.7.refs_2_ = bf16[128,896]{1,0:T(8,128)(2,1)S(1)} collective-permute-done((bf16[128,896]{1,0:T(8,128)(2,1)S(1)}, bf16[128,896]{1,0:T(8,128)(2,1)S(1)}, u32[]{:S(2)}, u32[]{:S(2)}) %collective-permute-start.7) | collective-permute-done | bytes 229408 | tf_op jit(solution)/shard_map/g3/ppermute | solution.py:283
  30.5 0.9 collective-permute-done.8.refs_1_
  31.4 19.8 %all_to_all.10.refs_1_ = bf16[16,8,896]{2,1,0:T(8,128)(2,1)S(1)} all-to-all(bf16[16,8,896]{2,1,0:T(8,128)(2,1)S(1)} %bitcast.12), channel_id=1, replica_groups=mesh['z'=8,'y'=4,'xh'=2,'xl'=2,'c'=2] {'z','xh'}, dimensions={0} | all-to-all | bytes 458752 | tf_op jit(solution)/shard_map/all_to_all | solution.py:348
  51.8 13.4 %all_to_all.11 = bf16[16,8,896]{2,1,0:T(8,128)(2,1)S(1)} all-to-all(bf16[16,8,896]{2,1,0:T(8,128)(2,1)S(1)} %shard_map.108), channel_id=1, replica_groups=mesh['z'=8,'y'=4,'xh'=2,'xl'=2,'c'=2] {'z','xh'}, dimensions={0} | all-to-all | bytes 458752 | tf_op jit(solution)/shard_map/all_to_all | solution.py:350
  65.2 3.1 %collective-permute-start.11 = (bf16[128,896]{1,0:T(8,128)(2,1)S(1)}, bf16[128,896]{1,0:T(8,128)(2,1)S(1)}, u32[]{:S(2)}, u32[]{:S(2)}) collective-permute-start(bf16[128,896]{1,0:T(8,128)(2,1)S(1)} %bitcast.5), channel_id=1, source_target_pairs={{0,24},{8,16},{16,8},{24,0},{1,25},{9,17},{17,9},{25,1},{2,26},{10... | collective-permute-start | bytes 688136 | tf_op jit(solution)/shard_map/e3/ppermute | solution.py:283
  69.0 4.9 %collective-permute-start.12 = (bf16[256,1024]{1,0:T(8,128)(2,1)S(1)}, bf16[256,1024]{1,0:T(8,128)(2,1)S(1)}, u32[]{:S(2)}, u32[]{:S(2)}) collective-permute-start(bf16[256,1024]{1,0:T(8,128)(2,1)S(1)} %shard_map.111), channel_id=1, source_target_pairs={{0,1},{1,0},{2,3},{3,2},{4,5},{5,4},{6,7},{7,6},{8,9},{9,8},{10,11... | collective-permute-start | bytes 1572872 | tf_op jit(solution)/shard_map/act_others/ppermute | solution.py:278
  75.5 5.1 %collective-permute-start.13 = (bf16[256,896]{1,0:T(8,128)(2,1)S(1)}, bf16[256,896]{1,0:T(8,128)(2,1)S(1)}, u32[]{:S(2)}, u32[]{:S(2)}) collective-permute-start(bf16[256,896]{1,0:T(8,128)(2,1)S(1)} %shard_map.112), channel_id=1, source_target_pairs={{0,1},{1,0},{2,3},{3,2},{4,5},{5,4},{6,7},{7,6},{8,9},{9,8},{10,11... | collective-permute-start | bytes 1376264 | tf_op jit(solution)/shard_map/err_others/ppermute | solution.py:278
  80.6 0.7 shard_map.109.refs_0_.refs_2_
  82.5 1.2 %collective-permute-start.15 = (bf16[128,1024]{1,0:T(8,128)(2,1)S(1)}, bf16[128,1024]{1,0:T(8,128)(2,1)S(1)}, u32[]{:S(2)}, u32[]{:S(2)}) collective-permute-start(bf16[128,1024]{1,0:T(8,128)(2,1)S(1)} %shard_map.110.refs_0_.refs_3_), channel_id=1, source_target_pairs={{0,2},{2,0},{1,3},{3,1},{4,6},{6,4},{5,7},{7,5},{8,10},{10,8},{9,1... | collective-permute-start | bytes 786440 | tf_op jit(solution)/shard_map/back0/ppermute | solution.py:278
  83.7 5.6 %collective-permute-done.14.refs_3_ = bf16[128,1024]{1,0:T(8,128)(2,1)S(1)} collective-permute-done((bf16[128,1024]{1,0:T(8,128)(2,1)S(1)}, bf16[128,1024]{1,0:T(8,128)(2,1)S(1)}, u32[]{:S(2)}, u32[]{:S(2)}) %collective-permute-start.14) | collective-permute-done | bytes 262176 | tf_op jit(solution)/shard_map/back1/ppermute | solution.py:278
  89.5 1.3 %collective-permute-start.17 = (bf16[128,1024]{1,0:T(8,128)(2,1)S(1)}, bf16[128,1024]{1,0:T(8,128)(2,1)S(1)}, u32[]{:S(2)}, u32[]{:S(2)}) collective-permute-start(bf16[128,1024]{1,0:T(8,128)(2,1)S(1)} %shard_map.114.refs_1_), channel_id=1, source_target_pairs={{0,1},{1,0},{2,3},{3,2},{4,5},{5,4},{6,7},{7,6},{8,9},{9,8},{10,11... | collective-permute-start | bytes 786440 | tf_op jit(solution)/shard_map/pre1o/ppermute | solution.py:278
  90.8 3.7 %shard_map.113 = (f32[1024,896]{1,0:T(8,128)}, f32[896]{0:T(1024)}, f32[8,128]{1,0:T(8,128)S(1)}) custom-call(bf16[128,1024]{1,0:T(8,128)(2,1)S(1)} %shard_map.110.refs_0_.refs_3_, bf16[128,1024]{1,0:T(8,128)(2,1)S(1)} %shard_map.102.refs_0_.refs_1_, bf16[128,1024]{1,0:T(8,128)(2,1)S(1)} %shard_map.104.refs_0_.refs_2_, ...), custom_call_target="tpu_custom_call" | custom-call | flops 1 | bytes 1 | tf_op jit(solution)/shard_map/pallas_call | solution.py:227
  95.1 0.9 collective-permute-start.16
  96.0 1.2 %collective-permute-done.16.refs_2_ = bf16[128,1024]{1,0:T(8,128)(2,1)S(1)} collective-permute-done((bf16[128,1024]{1,0:T(8,128)(2,1)S(1)}, bf16[128,1024]{1,0:T(8,128)(2,1)S(1)}, u32[]{:S(2)}, u32[]{:S(2)}) %collective-permute-start.16) | collective-permute-done | bytes 262176 | tf_op jit(solution)/shard_map/pre0o/ppermute | solution.py:278
  97.1 2.8 %shard_map.116 = (f32[896,1024]{1,0:T(8,128)}, f32[1024]{0:T(1024)}) custom-call(bf16[896,512]{1,0:T(8,128)(2,1)S(1)} %shard_map.95.refs_0_.t_ref, bf16[128,1024]{1,0:T(8,128)(2,1)S(1)} %shard_map.115.refs_0_, bf16[128,1024]{1,0:T(8,128)(2,1)S(1)} %shard_map.114.refs_1_, bf16[128,1024]{1,0:T(8,128)(2,1)S(1)} %collective-permute-done.16.refs_2_, ...), custom_call_target="tpu_custom_call" | custom-call | flops 1 | bytes 1 | tf_op jit(solution)/shard_map/pallas_call | solution.py:265
  (50 shorter events, 10.4 us)
Async XLA Ops:
  0.6 6.7 %copy-start = (bf16[896,1024]{1,0:T(8,128)(2,1)S(1)}, bf16[896,1024]{1,0:T(8,128)(2,1)}, u32[]{:S(2)}) copy-start(bf16[896,1024]{1,0:T(8,128)(2,1)} %refs_2_.2) | copy-start | bytes 5505028
  0.6 13.7 %collective-permute-start.2 = (bf16[1024,896]{1,0:T(8,128)(2,1)}, bf16[1024,896]{1,0:T(8,128)(2,1)}, u32[]{:S(2)}, u32[]{:S(2)}) collective-permute-start(bf16[1024,896]{1,0:T(8,128)(2,1)} %refs_1_.1), channel_id=1, source_target_pairs={{0,1},{1,0},{2,3},{3,2},{4,5},{5,4},{6,7},{7,6},{8,9},{9,8},{10,11... | collective-permute-start | bytes 5505032 | tf_op jit(solution)/shard_map/decoder2/ppermute | solution.py:278
  7.2 2.1 %copy-start.4 = (s32[2,16,1024]{2,1,0:T(8,128)S(1)}, s32[2,16,1024]{2,1,0:T(8,128)}, u32[]{:S(2)}) copy-start(s32[2,16,1024]{2,1,0:T(8,128)} %param.11) | copy-start | bytes 393220
  7.2 1.9 %collective-permute-start = (bf16[128,1024]{1,0:T(8,128)(2,1)S(1)}, bf16[128,1024]{1,0:T(8,128)(2,1)S(1)}, u32[]{:S(2)}, u32[]{:S(2)}) collective-permute-start(bf16[128,1024]{1,0:T(8,128)(2,1)S(1)} %get-tuple-element.27), channel_id=1, source_target_pairs={{0,1},{1,0},{2,3},{3,2},{4,5},{5,4},{6,7},{7,6},{8,9},{9,8},{10,11... | collective-permute-start | bytes 786440 | tf_op jit(solution)/shard_map/got0/ppermute | solution.py:278
  8.6 2.3 %collective-permute-start.1 = (bf16[128,1024]{1,0:T(8,128)(2,1)S(1)}, bf16[128,1024]{1,0:T(8,128)(2,1)S(1)}, u32[]{:S(2)}, u32[]{:S(2)}) collective-permute-start(bf16[128,1024]{1,0:T(8,128)(2,1)S(1)} %get-tuple-element.31), channel_id=1, source_target_pairs={{0,1},{1,0},{2,3},{3,2},{4,5},{5,4},{6,7},{7,6},{8,9},{9,8},{10,11... | collective-permute-start | bytes 786440 | tf_op jit(solution)/shard_map/got1/ppermute | solution.py:278
  9.2 8.0 %collective-permute-start.4 = (bf16[128,1024]{1,0:T(8,128)(2,1)S(1)}, bf16[128,1024]{1,0:T(8,128)(2,1)S(1)}, u32[]{:S(2)}, u32[]{:S(2)}) collective-permute-start(bf16[128,1024]{1,0:T(8,128)(2,1)S(1)} %shard_map.94.refs_0_.refs_4_), channel_id=1, source_target_pairs={{0,2},{2,0},{1,3},{3,1},{4,6},{6,4},{5,7},{7,5},{8,10},{10,8},{9,1... | collective-permute-start | bytes 786440 | tf_op jit(solution)/shard_map/away0/ppermute | solution.py:278
  9.3 3.2 %copy-start.3 = (f32[896]{0:T(1024)S(1)}, f32[896]{0:T(1024)}, u32[]{:S(2)}) copy-start(f32[896]{0:T(1024)} %refs_2_.3) | copy-start | bytes 10756
  10.2 3.6 %copy-start.1 = (bf16[1024,896]{1,0:T(8,128)(2,1)S(1)}, bf16[1024,896]{1,0:T(8,128)(2,1)}, u32[]{:S(2)}) copy-start(bf16[1024,896]{1,0:T(8,128)(2,1)} %refs_1_.1) | copy-start | bytes 5505028
  10.9 11.8 %collective-permute-start.5 = (bf16[128,1024]{1,0:T(8,128)(2,1)S(1)}, bf16[128,1024]{1,0:T(8,128)(2,1)S(1)}, u32[]{:S(2)}, u32[]{:S(2)}) collective-permute-start(bf16[128,1024]{1,0:T(8,128)(2,1)S(1)} %shard_map.98.refs_0_.refs_2_), channel_id=1, source_target_pairs={{0,2},{2,0},{1,3},{3,1},{4,6},{6,4},{5,7},{7,5},{8,10},{10,8},{9,1... | collective-permute-start | bytes 786440 | tf_op jit(solution)/shard_map/away1/ppermute | solution.py:278
  13.0 4.1 %copy-start.2 = (f32[1024]{0:T(1024)S(1)}, f32[1024]{0:T(1024)}, u32[]{:S(2)}) copy-start(f32[1024]{0:T(1024)} %refs_4_.1) | copy-start | bytes 12292
  13.1 3.4 %collective-permute-start.3 = (f32[8,896]{1,0:T(8,128)S(1)}, f32[8,896]{1,0:T(8,128)S(1)}, u32[]{:S(2)}, u32[]{:S(2)}) collective-permute-start(f32[8,896]{1,0:T(8,128)S(1)} %get-tuple-element.34), channel_id=1, source_target_pairs={{0,1},{1,0},{2,3},{3,2},{4,5},{5,4},{6,7},{7,6},{8,9},{9,8},{10,11... | collective-permute-start | bytes 86024 | tf_op jit(solution)/shard_map/base2/ppermute | solution.py:278
  18.0 12.4 %collective-permute-start.7 = (bf16[128,896]{1,0:T(8,128)(2,1)S(1)}, bf16[128,896]{1,0:T(8,128)(2,1)S(1)}, u32[]{:S(2)}, u32[]{:S(2)}) collective-permute-start(bf16[128,896]{1,0:T(8,128)(2,1)S(1)} %get-tuple-element.40), channel_id=1, source_target_pairs={{0,24},{8,16},{16,8},{24,0},{1,25},{9,17},{17,9},{25,1},{2,26},{10... | collective-permute-start | bytes 688136 | tf_op jit(solution)/shard_map/g3/ppermute | solution.py:283
  19.1 11.3 %collective-permute-start.6 = (bf16[128,896]{1,0:T(8,128)(2,1)S(1)}, bf16[128,896]{1,0:T(8,128)(2,1)S(1)}, u32[]{:S(2)}, u32[]{:S(2)}) collective-permute-start(bf16[128,896]{1,0:T(8,128)(2,1)S(1)} %get-tuple-element.37.refs_0_), channel_id=1, source_target_pairs={{0,16},{8,24},{16,0},{24,8},{1,17},{9,25},{17,1},{25,9},{2,18},{10... | collective-permute-start | bytes 688136 | tf_op jit(solution)/shard_map/g2/ppermute | solution.py:283
  23.6 7.8 %collective-permute-start.8 = (bf16[128,896]{1,0:T(8,128)(2,1)S(1)}, bf16[128,896]{1,0:T(8,128)(2,1)S(1)}, u32[]{:S(2)}, u32[]{:S(2)}) collective-permute-start(bf16[128,896]{1,0:T(8,128)(2,1)S(1)} %get-tuple-element.41), channel_id=1, source_target_pairs={{0,8},{8,0},{16,24},{24,16},{1,9},{9,1},{17,25},{25,17},{2,10},{10... | collective-permute-start | bytes 688136 | tf_op jit(solution)/shard_map/g1/ppermute | solution.py:283
  65.2 9.3 %collective-permute-start.11 = (bf16[128,896]{1,0:T(8,128)(2,1)S(1)}, bf16[128,896]{1,0:T(8,128)(2,1)S(1)}, u32[]{:S(2)}, u32[]{:S(2)}) collective-permute-start(bf16[128,896]{1,0:T(8,128)(2,1)S(1)} %bitcast.5), channel_id=1, source_target_pairs={{0,24},{8,16},{16,8},{24,0},{1,25},{9,17},{17,9},{25,1},{2,26},{10... | collective-permute-start | bytes 688136 | tf_op jit(solution)/shard_map/e3/ppermute | solution.py:283
  68.4 6.5 %collective-permute-start.10 = (bf16[128,896]{1,0:T(8,128)(2,1)S(1)}, bf16[128,896]{1,0:T(8,128)(2,1)S(1)}, u32[]{:S(2)}, u32[]{:S(2)}) collective-permute-start(bf16[128,896]{1,0:T(8,128)(2,1)S(1)} %bitcast.6), channel_id=1, source_target_pairs={{0,16},{8,24},{16,0},{24,8},{1,17},{9,25},{17,1},{25,9},{2,18},{10... | collective-permute-start | bytes 688136 | tf_op jit(solution)/shard_map/e2/ppermute | solution.py:283
  68.7 6.8 %collective-permute-start.9 = (bf16[128,896]{1,0:T(8,128)(2,1)S(1)}, bf16[128,896]{1,0:T(8,128)(2,1)S(1)}, u32[]{:S(2)}, u32[]{:S(2)}) collective-permute-start(bf16[128,896]{1,0:T(8,128)(2,1)S(1)} %bitcast.7), channel_id=1, source_target_pairs={{0,8},{8,0},{16,24},{24,16},{1,9},{9,1},{17,25},{25,17},{2,10},{10... | collective-permute-start | bytes 688136 | tf_op jit(solution)/shard_map/e1/ppermute | solution.py:283
  69.0 21.8 %collective-permute-start.12 = (bf16[256,1024]{1,0:T(8,128)(2,1)S(1)}, bf16[256,1024]{1,0:T(8,128)(2,1)S(1)}, u32[]{:S(2)}, u32[]{:S(2)}) collective-permute-start(bf16[256,1024]{1,0:T(8,128)(2,1)S(1)} %shard_map.111), channel_id=1, source_target_pairs={{0,1},{1,0},{2,3},{3,2},{4,5},{5,4},{6,7},{7,6},{8,9},{9,8},{10,11... | collective-permute-start | bytes 1572872 | tf_op jit(solution)/shard_map/act_others/ppermute | solution.py:278
  75.5 15.2 %collective-permute-start.13 = (bf16[256,896]{1,0:T(8,128)(2,1)S(1)}, bf16[256,896]{1,0:T(8,128)(2,1)S(1)}, u32[]{:S(2)}, u32[]{:S(2)}) collective-permute-start(bf16[256,896]{1,0:T(8,128)(2,1)S(1)} %shard_map.112), channel_id=1, source_target_pairs={{0,1},{1,0},{2,3},{3,2},{4,5},{5,4},{6,7},{7,6},{8,9},{9,8},{10,11... | collective-permute-start | bytes 1376264 | tf_op jit(solution)/shard_map/err_others/ppermute | solution.py:278
  81.4 8.0 %collective-permute-start.14 = (bf16[128,1024]{1,0:T(8,128)(2,1)S(1)}, bf16[128,1024]{1,0:T(8,128)(2,1)S(1)}, u32[]{:S(2)}, u32[]{:S(2)}) collective-permute-start(bf16[128,1024]{1,0:T(8,128)(2,1)S(1)} %shard_map.109.refs_0_.refs_2_), channel_id=1, source_target_pairs={{0,2},{2,0},{1,3},{3,1},{4,6},{6,4},{5,7},{7,5},{8,10},{10,8},{9,1... | collective-permute-start | bytes 786440 | tf_op jit(solution)/shard_map/back1/ppermute | solution.py:278
  82.5 12.5 %collective-permute-start.15 = (bf16[128,1024]{1,0:T(8,128)(2,1)S(1)}, bf16[128,1024]{1,0:T(8,128)(2,1)S(1)}, u32[]{:S(2)}, u32[]{:S(2)}) collective-permute-start(bf16[128,1024]{1,0:T(8,128)(2,1)S(1)} %shard_map.110.refs_0_.refs_3_), channel_id=1, source_target_pairs={{0,2},{2,0},{1,3},{3,1},{4,6},{6,4},{5,7},{7,5},{8,10},{10,8},{9,1... | collective-permute-start | bytes 786440 | tf_op jit(solution)/shard_map/back0/ppermute | solution.py:278
  89.5 6.5 %collective-permute-start.17 = (bf16[128,1024]{1,0:T(8,128)(2,1)S(1)}, bf16[128,1024]{1,0:T(8,128)(2,1)S(1)}, u32[]{:S(2)}, u32[]{:S(2)}) collective-permute-start(bf16[128,1024]{1,0:T(8,128)(2,1)S(1)} %shard_map.114.refs_1_), channel_id=1, source_target_pairs={{0,1},{1,0},{2,3},{3,2},{4,5},{5,4},{6,7},{7,6},{8,9},{9,8},{10,11... | collective-permute-start | bytes 786440 | tf_op jit(solution)/shard_map/pre1o/ppermute | solution.py:278
  95.1 2.1 %collective-permute-start.16 = (bf16[128,1024]{1,0:T(8,128)(2,1)S(1)}, bf16[128,1024]{1,0:T(8,128)(2,1)S(1)}, u32[]{:S(2)}, u32[]{:S(2)}) collective-permute-start(bf16[128,1024]{1,0:T(8,128)(2,1)S(1)} %shard_map.115.refs_0_), channel_id=1, source_target_pairs={{0,1},{1,0},{2,3},{3,2},{4,5},{5,4},{6,7},{7,6},{8,9},{9,8},{10,11... | collective-permute-start | bytes 786440 | tf_op jit(solution)/shard_map/pre0o/ppermute | solution.py:278

commit v3 on v2

--- a/solution.py
+++ b/solution.py
@@ -117,12 +117,17 @@
     return call(kernel, [(chip.shape, bf16)], (gate, chip, away, bias), None, after)[0]
 
 
-def gradient(gate, chip, away, after=()):
-    def kernel(gate_ref, chip_ref, away_ref, out_ref):
-        value = chip_ref[...].astype(f32) + away_ref[...].astype(f32)
-        out_ref[...] = (value * gate_ref[...].astype(f32)).astype(bf16)
-
-    return call(kernel, [(chip.shape, bf16)], (gate, chip, away), None, after)[0]
+def gradient(gate, chips, aways, after=()):
+    count = len(chips)
+    rows = chips[0].shape[0]
+
+    def kernel(gate_ref, *refs):
+        for k in range(count):
+            at = slice(k * rows, k * rows + rows)
+            value = refs[k][...].astype(f32) + refs[count + k][...].astype(f32)
+            refs[-1][at] = (value * gate_ref[at].astype(f32)).astype(bf16)
+
+    return call(kernel, [(gate.shape, bf16)], (gate, *chips, *aways), None, after)[0]
 
 
 def decode(own, dec_own, dec_other, after=()):
@@ -163,19 +168,23 @@
     return call(kernel, [(pieces.shape, bf16)], (pieces, own, other), ids)[0]
 
 
-def back(errs, dec_own, dec_other, after=()):
+def back(errs, dec_own, dec_other, sizes, after=()):
     n = dec_own.shape[1]
     count = len(errs)
 
     def kernel(*refs):
-        dec_ref, oth_ref, out_ref = refs[count:]
+        dec_ref, oth_ref = refs[count:count + 2]
         own = jnp.concatenate([ref[:Q] for ref in refs[:count]], axis=0)
         other = jnp.concatenate([ref[Q:] for ref in refs[:count]], axis=0)
         out = jnp.dot(own, dec_ref[...], preferred_element_type=f32)
         out = out + jnp.dot(other, oth_ref[...], preferred_element_type=f32)
-        out_ref[...] = out.astype(bf16)
-
-    return call(kernel, [((count * Q, n), bf16)], (*errs, dec_own, dec_other), None, after)[0]
+        out = out.astype(bf16)
+        at = 0
+        for size, ref in zip(sizes, refs[count + 2:]):
+            ref[...] = out[at:at + size * Q]
+            at += size * Q
+
+    return call(kernel, [((size * Q, n), bf16) for size in sizes], (*errs, dec_own, dec_other), None, after)
 
 
 def flipped(x, after):
@@ -202,75 +211,50 @@
     return call(kernel, [((d, 4 * CHUNK), bf16)], (tokens,), ids, after)[0]
 
 
-def decoder_grad(owns, others, errs, err_others, after):
-    n, d = others.shape[1], errs[0].shape[1]
-    tile = 256
+def columns(parts, n, after):
+    rows = sum(x.shape[0] for x in parts)
+    shape = (n, rows)
+
+    def kernel(*refs):
+        whole = jnp.concatenate([ref[:, :n] for ref in refs[:-1]], axis=0)
+        for at in range(0, rows, CHUNK):
+            refs[-1][:, at:at + CHUNK] = whole[at:at + CHUNK].T
+
+    return call(kernel, [(shape, bf16)], parts, None, after)[0]
+
+
+def product(lefts, parts, after=()):
+    d, n = lefts[0].shape[0], parts[0][0].shape[1]
+    pieces = d // CHUNK
+    count = len(parts)
     skip = len(after)
-    rows = len(ORDER) * Q
+    wide = len(lefts)
 
     def kernel(*refs):
-        a0, a1, a2, e0, e1, e2, e3, other, out_ref, sum_ref, done_ref, err_ref = refs[skip:]
-
-        @pl.when(pl.program_id(0) == 0)
-        def _():
-            e = (e0, e1, e2, e3)
-            for k, r in enumerate(ORDER):
-                err_ref[k * Q:k * Q + Q] = e[r][:Q]
-            err_ref[rows:] = other[...]
-            sum_ref[...] = jnp.sum(err_ref[...].astype(f32), axis=0)
-            done_ref[...] = jnp.zeros_like(done_ref)
-
-        lhs = jnp.concatenate([a0[...], a1[...], a2[...]], axis=0)
-        out_ref[...] = lax.dot_general(lhs, err_ref[...], DOWN, preferred_element_type=f32)
-
-    acts = (*owns, others)
+        left_refs, refs = refs[skip:skip + wide], refs[skip + wide:]
+        out_hbm, sum_ref, done_ref, out, sems = refs[count:]
+        right = jnp.concatenate([ref[:rows, -n:] for ref, (_, rows) in zip(refs, parts)], axis=0)
+        copies = []
+        for k in range(pieces):
+            rows = pl.ds(k * CHUNK, CHUNK)
+            left = jnp.concatenate([ref[rows] for ref in left_refs], axis=1)
+            out[rows] = jnp.dot(left, right, preferred_element_type=f32)
+            copies.append(pltpu.make_async_copy(out.at[rows], out_hbm.at[rows], sems.at[k]))
+            copies[-1].start()
+        sum_ref[...] = jnp.dot(jnp.ones((16, right.shape[0]), bf16), right, preferred_element_type=f32)[0]
+        done_ref[...] = jnp.zeros_like(done_ref)
+        for copy in copies:
+            copy.wait()
+
     return pl.pallas_call(
         kernel,
-        grid=(n // tile,),
-        in_specs=[ANY] * skip
-        + [pl.BlockSpec((act.shape[0], tile), lambda i: (0, i)) for act in acts]
-        + [pl.BlockSpec((CHUNK, d), lambda i: (0, 0))] * 4
-        + [pl.BlockSpec((rows, d), lambda i: (0, 0))],
-        out_specs=[
-            pl.BlockSpec((tile, d), lambda i: (i, 0)),
-            pl.BlockSpec((d,), lambda i: (0,)),
-            pl.BlockSpec((8, 128), lambda i: (0, 0)),
-        ],
-        out_shape=[jax.ShapeDtypeStruct((n, d), f32), jax.ShapeDtypeStruct((d,), f32), jax.ShapeDtypeStruct((8, 128), f32)],
-        scratch_shapes=[pltpu.VMEM((2 * rows, d), bf16)],
+        in_specs=[ANY] * skip + [VMEM] * (wide + count),
+        out_specs=[ANY, VMEM, VMEM],
+        out_shape=[jax.ShapeDtypeStruct(s, f32) for s in ((d, n), (n,), (8, 128))],
+        scratch_shapes=[pltpu.VMEM((d, n), f32), pltpu.SemaphoreType.DMA((pieces,))],
         compiler_params=pltpu.CompilerParams(vmem_limit_bytes=24 << 20),
         cost_estimate=TINY,
-    )(*after, *acts, *errs, err_others)
-
-
-def encoder_grad(tok_t, pres):
-    d, n = tok_t.shape[0], pres[0].shape[1]
-    parts = 7
-    tile = d // parts
-    count = len(pres)
-
-    def kernel(t_ref, *refs):
-        out_hbm, sum_ref, out, sems = refs[count:]
-        pre = jnp.concatenate([ref[...] for ref in refs[:count]], axis=0)
-        copies = []
-        for k in range(parts):
-            rows = pl.ds(k * tile, tile)
-            out[rows] = jnp.dot(t_ref[rows], pre, preferred_element_type=f32)
-            copies.append(pltpu.make_async_copy(out.at[rows], out_hbm.at[rows], sems.at[k]))
-            copies[-1].start()
-        sum_ref[...] = jnp.dot(jnp.ones((16, 4 * CHUNK), bf16), pre, preferred_element_type=f32)[0]
-        for copy in copies:
-            copy.wait()
-
-    return pl.pallas_call(
-        kernel,
-        in_specs=[VMEM] * (1 + count),
-        out_specs=[ANY, VMEM],
-        out_shape=[jax.ShapeDtypeStruct((d, n), f32), jax.ShapeDtypeStruct((n,), f32)],
-        scratch_shapes=[pltpu.VMEM((d, n), f32), pltpu.SemaphoreType.DMA((parts,))],
-        compiler_params=pltpu.CompilerParams(vmem_limit_bytes=24 << 20),
-        cost_estimate=TINY,
-    )(tok_t, *pres)
+    )(*after, *lefts, *[x for x, _ in parts])
 
 
 def swap(x, axis, name):
@@ -290,17 +274,17 @@
     return call(kernel, [(a.shape, bf16)], (a, b), None, after)[0]
 
 
-def stacked(parts, after=()):
-    rows = [x.shape[0] - at for x, at in parts]
+def split(errs, acts, after):
+    count = len(errs)
+    n, d = acts[0][0].shape[1], errs[0][0].shape[1]
 
     def kernel(*refs):
-        at = 0
-        for (_, start), size, ref in zip(parts, rows, refs):
-            refs[-1][at:at + size] = ref[start:]
-            at += size
-
-    shape = ((sum(rows), parts[0][0].shape[1]), bf16)
-    return call(kernel, [shape], [x for x, _ in parts], None, after)[0]
+        for k in range(count):
+            refs[2 * count + k][:, :n] = refs[count + k][acts[k][1]:acts[k][1] + Q]
+            refs[2 * count + k][:, n:] = refs[k][errs[k][1]:errs[k][1] + Q]
+
+    args = [x for x, _ in errs] + [x for x, _ in acts]
+    return call(kernel, [((Q, n + d), bf16)] * count, args, None, after)
 
 
 def add3(a, b, c):
@@ -349,18 +333,21 @@
     copies = error(ids, pieces, base, base2)
     e0 = lax.all_to_all(copies, FAR, 0, 0).reshape(CHUNK, d)
     e1, e3, e2 = partner(e0, 1, "e1"), partner(e0, 3, "e3"), partner(e0, 2, "e2")
-    part1 = back([e1, e0], dec_t, dec_t2)
-    away1 = swap(part1, "xl", "back1")
-    part0 = back([e2, e3], dec_t, dec_t2, [part1])
-    away0 = swap(part0, "xl", "back0")
-    act_others = swap(stacked([(act0, 0), (act1, 0)], [e0]), "c", "act_others")
-    err_others = swap(stacked([(e2, Q), (e3, Q), (e1, Q), (e0, Q)]), "c", "err_others")
-    pre1 = gradient(gate1, part1, away1, [part0])
+    part1 = back([e1, e0], dec_t, dec_t2, [1, 1])
+    away1 = [swap(part, "xl", "back1") for part in part1]
+    part0 = back([e2, e3], dec_t, dec_t2, [2], part1[:1])
+    away0 = [swap(part, "xl", "back0") for part in part0]
+    act_own = columns([act0, act1], act0.shape[1], part0)
+    moved = split([(e2, Q), (e3, Q), (e1, Q), (e0, Q)], [(act0, 0), (act0, Q), (act1, 0), (act1, Q)], [act_own])
+    moved = [swap(x, "c", "moved") for x in moved]
+    pre1 = gradient(gate1, part1, away1, [act_own])
     pre1o = swap(pre1, "c", "pre1o")
-    grad_dec, dec_sum, done = decoder_grad((act0, act1), act_others, (e0, e1, e2, e3), err_others, [part0])
-    pre0 = gradient(gate0, part0, away0, [done, pre1])
+    act_other = columns(moved, act0.shape[1], [pre1])
+    errs = [(e2, Q), (e3, Q), (e1, Q), (e0, Q)] + [(x, Q) for x in moved]
+    pre0 = gradient(gate0, part0, away0, [act_other])
     pre0o = swap(pre0, "c", "pre0o")
-    grad_enc, enc_sum = encoder_grad(tok_t, [pre0, pre1, pre0o, pre1o])
+    grad_dec, dec_sum, done = product([act_own, act_other], errs, [pre0])
+    grad_enc, enc_sum, _ = product([tok_t], [(x, CHUNK) for x in (pre0, pre1, pre0o, pre1o)], [done])
     return grad_enc, grad_dec, enc_sum, dec_sum
 
 

time: 100 us -> 94.6 us (0.946)
  waiting for transfers between devices: 20.5 us -> 16.6 us
  starting transfers between devices: 25.4 us -> 24.1 us
    ppermute x12 -> x15, waiting for transfers between devices: 11.4 us -> 4.91 us  [swap(): return lax.ppermute(x, axis, SWAP)]
    ppermute x6, waiting for transfers between devices: 9.19 us -> 11.7 us  [partner(): return lax.ppermute(x, 'y', [(i, i ^ r) for i in range(4)])]
    ppermute x12 -> x15, starting transfers between devices: 20.2 us -> 18.2 us  [swap(): return lax.ppermute(x, axis, SWAP)]
    pallas_call x21 -> x22, Pallas kernels: 10.2 us -> 10.6 us  [call(): pl.pallas_call(body, out_shape=[jax.ShapeDtypeStruct(s, t) for s, t in ou...]
  transfers between devices with their start and end apart: 18 -> 21, of which waited for: 10 -> 8; matrix products, arithmetic and copies ran while one was open for 0% -> 0% of each run, Pallas kernels for 16% -> 17%
where the time goes in v3:
time: 94.6 us; the launch traced here: 94.4 us
  blocking collectives  33.2 us (35%)
  starting transfers between devices  24.1 us (25%)
  Pallas kernels  19.3 us (20%)
  waiting for transfers between devices  16.6 us (18%)
  between operations  1.11 us (1%)
    all_to_all x1, blocking collectives, shards(): pieces = lax.all_to_all(total.reshape(PEERS, ROWS, d), FAR, 0, 0)  19.8 us
    ppermute x15, starting transfers between devices, swap(): return lax.ppermute(x, axis, SWAP)  18.2 us
    all_to_all x1, blocking collectives, shards(): e0 = lax.all_to_all(copies, FAR, 0, 0).reshape(CHUNK, d)  13.4 us
    ppermute x6, waiting for transfers between devices, partner(): return lax.ppermute(x, 'y', [(i, i ^ r) for i in range(4)])  11.7 us
    pallas_call x22, Pallas kernels, call(): pl.pallas_call(body, out_shape=[jax.ShapeDtypeStruct(s, t) for s, t in ou...  10.6 us
    ppermute x6, starting transfers between devices, partner(): return lax.ppermute(x, 'y', [(i, i ^ r) for i in range(4)])  5.85 us
    pallas_call x2, Pallas kernels, product(): pl.pallas_call(kernel, in_specs=[ANY] * skip + [VMEM] * (wide + count), o...  5.59 us
    ppermute x15, waiting for transfers between devices, swap(): return lax.ppermute(x, axis, SWAP)  4.91 us
  transfers between devices with their start and end apart: 21, of which 8 were waited for; matrix products, arithmetic and copies ran while one was open for 0% of the time, Pallas kernels for 17%

profile of v3, /device:TPU:1, one launch (start us, length us, event | category | flops | bytes accessed | tf_op | source)
XLA Modules:
  0.0 94.4 jit_solution(12607672208902749033)
XLA Ops:
  0.6 3.3 %collective-permute-start.2 = (bf16[1024,896]{1,0:T(8,128)(2,1)}, bf16[1024,896]{1,0:T(8,128)(2,1)}, u32[]{:S(2)}, u32[]{:S(2)}) collective-permute-start(bf16[1024,896]{1,0:T(8,128)(2,1)} %refs_1_.1), channel_id=1, source_target_pairs={{0,1},{1,0},{2,3},{3,2},{4,5},{5,4},{6,7},{7,6},{8,9},{9,8},{10,11... | collective-permute-start | bytes 5505032 | tf_op jit(solution)/shard_map/decoder2/ppermute | solution.py:262
  4.0 3.2 %shard_map.93 = (bf16[128,1024]{1,0:T(8,128)(2,1)S(1)}, bf16[128,1024]{1,0:T(8,128)(2,1)S(1)}, bf16[8,64,896]{2,1,0:T(8,128)(2,1)S(1)}) custom-call(s32[11]{0:T(128)S(1)} %compare_select_fusion.1.ids_ref.refs_1_.refs_0_, bf16[8,64,896]{2,1,0:T(8,128)(2,1)} %bitcast.12, bf16[896,1024]{1,0:T(8,128)(2,1)} %refs_2_.2), custom_call_target="tpu_custom_call" | custom-call | flops 1 | bytes 1 | tf_op jit(solution)/shard_map/pallas_call | solution.py:69
  7.3 1.2 %shard_map.97 = (bf16[128,1024]{1,0:T(8,128)(2,1)S(1)}, bf16[128,1024]{1,0:T(8,128)(2,1)S(1)}) custom-call(s32[11]{0:T(128)S(1)} %compare_select_fusion.1.ids_ref.refs_1_.refs_0_, bf16[8,64,896]{2,1,0:T(8,128)(2,1)S(1)} %get-tuple-element.34.refs_2_.refs_1_, bf16[896,1024]{1,0:T(8,128)(2,1)S(1)} %copy-done), custom_call_target="tpu_custom_call" | custom-call | flops 1 | bytes 1 | tf_op jit(solution)/shard_map/pallas_call | solution.py:37
  10.9 1.5 %collective-permute-start.5 = (bf16[128,1024]{1,0:T(8,128)(2,1)S(1)}, bf16[128,1024]{1,0:T(8,128)(2,1)S(1)}, u32[]{:S(2)}, u32[]{:S(2)}) collective-permute-start(bf16[128,1024]{1,0:T(8,128)(2,1)S(1)} %shard_map.98.refs_0_.refs_2_), channel_id=1, source_target_pairs={{0,2},{2,0},{1,3},{3,1},{4,6},{6,4},{5,7},{7,5},{8,10},{10,8},{9,1... | collective-permute-start | bytes 786440 | tf_op jit(solution)/shard_map/away1/ppermute | solution.py:262
  14.4 2.1 %shard_map.100 = (bf16[896,1024]{1,0:T(8,128)(2,1)S(1)}, bf16[1024,896]{1,0:T(8,128)(2,1)S(1)}) custom-call(bf16[128,1024]{1,0:T(8,128)(2,1)S(1)} %shard_map.98.refs_0_.refs_2_, bf16[1024,896]{1,0:T(8,128)(2,1)} %collective-permute-done.2.refs_1_), custom_call_target="tpu_custom_call" | custom-call | flops 1 | bytes 1 | tf_op jit(solution)/shard_map/pallas_call | solution.py:37
  18.0 1.1 %collective-permute-start.7 = (bf16[128,896]{1,0:T(8,128)(2,1)S(1)}, bf16[128,896]{1,0:T(8,128)(2,1)S(1)}, u32[]{:S(2)}, u32[]{:S(2)}) collective-permute-start(bf16[128,896]{1,0:T(8,128)(2,1)S(1)} %get-tuple-element.46), channel_id=1, source_target_pairs={{0,24},{8,16},{16,8},{24,0},{1,25},{9,17},{17,9},{25,1},{2,26},{10... | collective-permute-start | bytes 688136 | tf_op jit(solution)/shard_map/g3/ppermute | solution.py:267
  19.4 3.3 %collective-permute-done.5.refs_3_ = bf16[128,1024]{1,0:T(8,128)(2,1)S(1)} collective-permute-done((bf16[128,1024]{1,0:T(8,128)(2,1)S(1)}, bf16[128,1024]{1,0:T(8,128)(2,1)S(1)}, u32[]{:S(2)}, u32[]{:S(2)}) %collective-permute-start.5) | collective-permute-done | bytes 262176 | tf_op jit(solution)/shard_map/away1/ppermute | solution.py:262
  23.7 6.7 %collective-permute-done.7.refs_2_ = bf16[128,896]{1,0:T(8,128)(2,1)S(1)} collective-permute-done((bf16[128,896]{1,0:T(8,128)(2,1)S(1)}, bf16[128,896]{1,0:T(8,128)(2,1)S(1)}, u32[]{:S(2)}, u32[]{:S(2)}) %collective-permute-start.7) | collective-permute-done | bytes 229408 | tf_op jit(solution)/shard_map/g3/ppermute | solution.py:267
  30.5 0.9 collective-permute-done.8.refs_1_
  31.4 19.8 %all_to_all.10.refs_1_ = bf16[16,8,896]{2,1,0:T(8,128)(2,1)S(1)} all-to-all(bf16[16,8,896]{2,1,0:T(8,128)(2,1)S(1)} %bitcast.11), channel_id=1, replica_groups=mesh['z'=8,'y'=4,'xh'=2,'xl'=2,'c'=2] {'z','xh'}, dimensions={0} | all-to-all | bytes 458752 | tf_op jit(solution)/shard_map/all_to_all | solution.py:332
  51.8 13.4 %all_to_all.11 = bf16[16,8,896]{2,1,0:T(8,128)(2,1)S(1)} all-to-all(bf16[16,8,896]{2,1,0:T(8,128)(2,1)S(1)} %shard_map.108), channel_id=1, replica_groups=mesh['z'=8,'y'=4,'xh'=2,'xl'=2,'c'=2] {'z','xh'}, dimensions={0} | all-to-all | bytes 458752 | tf_op jit(solution)/shard_map/all_to_all | solution.py:334
  65.2 1.7 %collective-permute-start.9 = (bf16[128,896]{1,0:T(8,128)(2,1)S(1)}, bf16[128,896]{1,0:T(8,128)(2,1)S(1)}, u32[]{:S(2)}, u32[]{:S(2)}) collective-permute-start(bf16[128,896]{1,0:T(8,128)(2,1)S(1)} %bitcast.5), channel_id=1, source_target_pairs={{0,8},{8,0},{16,24},{24,16},{1,9},{9,1},{17,25},{25,17},{2,10},{10... | collective-permute-start | bytes 688136 | tf_op jit(solution)/shard_map/e1/ppermute | solution.py:267
  67.0 1.8 %collective-permute-start.11 = (bf16[128,896]{1,0:T(8,128)(2,1)S(1)}, bf16[128,896]{1,0:T(8,128)(2,1)S(1)}, u32[]{:S(2)}, u32[]{:S(2)}) collective-permute-start(bf16[128,896]{1,0:T(8,128)(2,1)S(1)} %bitcast.6), channel_id=1, source_target_pairs={{0,24},{8,16},{16,8},{24,0},{1,25},{9,17},{17,9},{25,1},{2,26},{10... | collective-permute-start | bytes 688136 | tf_op jit(solution)/shard_map/e3/ppermute | solution.py:267
  69.6 0.8 collective-permute-done.9.refs_0_.refs_3_.refs_5_
  71.7 1.2 %collective-permute-start.12 = (bf16[64,1024]{1,0:T(8,128)(2,1)S(1)}, bf16[64,1024]{1,0:T(8,128)(2,1)S(1)}, u32[]{:S(2)}, u32[]{:S(2)}) collective-permute-start(bf16[64,1024]{1,0:T(8,128)(2,1)S(1)} %get-tuple-element.49.refs_0_.refs_2_), channel_id=1, source_target_pairs={{0,2},{2,0},{1,3},{3,1},{4,6},{6,4},{5,7},{7,5},{8,10},{10,8},{9,1... | collective-permute-start | bytes 393224 | tf_op jit(solution)/shard_map/back1/ppermute | solution.py:262
  72.9 2.1 %collective-permute-done.11.refs_2_.refs_4_ = bf16[128,896]{1,0:T(8,128)(2,1)S(1)} collective-permute-done((bf16[128,896]{1,0:T(8,128)(2,1)S(1)}, bf16[128,896]{1,0:T(8,128)(2,1)S(1)}, u32[]{:S(2)}, u32[]{:S(2)}) %collective-permute-start.11) | collective-permute-done | bytes 229408 | tf_op jit(solution)/shard_map/e3/ppermute | solution.py:267
  74.9 1.2 %collective-permute-done.10.refs_1_.refs_3_ = bf16[128,896]{1,0:T(8,128)(2,1)S(1)} collective-permute-done((bf16[128,896]{1,0:T(8,128)(2,1)S(1)}, bf16[128,896]{1,0:T(8,128)(2,1)S(1)}, u32[]{:S(2)}, u32[]{:S(2)}) %collective-permute-start.10) | collective-permute-done | bytes 229408 | tf_op jit(solution)/shard_map/e2/ppermute | solution.py:267
  77.4 5.5 %collective-permute-start.14 = (bf16[64,1920]{1,0:T(8,128)(2,1)S(1)}, bf16[64,1920]{1,0:T(8,128)(2,1)S(1)}, u32[]{:S(2)}, u32[]{:S(2)}) collective-permute-start(bf16[64,1920]{1,0:T(8,128)(2,1)S(1)} %get-tuple-element.51), channel_id=1, source_target_pairs={{0,1},{1,0},{2,3},{3,2},{4,5},{5,4},{6,7},{7,6},{8,9},{9,8},{10,11... | collective-permute-start | bytes 737288 | tf_op jit(solution)/shard_map/moved/ppermute | solution.py:262
  83.0 1.2 %collective-permute-start.16 = (bf16[64,1920]{1,0:T(8,128)(2,1)S(1)}, bf16[64,1920]{1,0:T(8,128)(2,1)S(1)}, u32[]{:S(2)}, u32[]{:S(2)}) collective-permute-start(bf16[64,1920]{1,0:T(8,128)(2,1)S(1)} %get-tuple-element.53), channel_id=1, source_target_pairs={{0,1},{1,0},{2,3},{3,2},{4,5},{5,4},{6,7},{7,6},{8,9},{9,8},{10,11... | collective-permute-start | bytes 737288 | tf_op jit(solution)/shard_map/moved/ppermute | solution.py:262
  84.2 1.4 %collective-permute-start.17 = (bf16[64,1920]{1,0:T(8,128)(2,1)S(1)}, bf16[64,1920]{1,0:T(8,128)(2,1)S(1)}, u32[]{:S(2)}, u32[]{:S(2)}) collective-permute-start(bf16[64,1920]{1,0:T(8,128)(2,1)S(1)} %get-tuple-element.54), channel_id=1, source_target_pairs={{0,1},{1,0},{2,3},{3,2},{4,5},{5,4},{6,7},{7,6},{8,9},{9,8},{10,11... | collective-permute-start | bytes 737288 | tf_op jit(solution)/shard_map/moved/ppermute | solution.py:262
  85.9 0.9 collective-permute-done.17.refs_4_.refs_10_
  87.1 1.5 %collective-permute-start.19 = (bf16[128,1024]{1,0:T(8,128)(2,1)S(1)}, bf16[128,1024]{1,0:T(8,128)(2,1)S(1)}, u32[]{:S(2)}, u32[]{:S(2)}) collective-permute-start(bf16[128,1024]{1,0:T(8,128)(2,1)S(1)} %shard_map.115.refs_0_.refs_2_), channel_id=1, source_target_pairs={{0,1},{1,0},{2,3},{3,2},{4,5},{5,4},{6,7},{7,6},{8,9},{9,8},{10,11... | collective-permute-start | bytes 786440 | tf_op jit(solution)/shard_map/pre0o/ppermute | solution.py:262
  88.6 2.8 %shard_map.116 = (f32[1024,896]{1,0:T(8,128)}, f32[896]{0:T(1024)}, f32[8,128]{1,0:T(8,128)S(1)}) custom-call(bf16[128,1024]{1,0:T(8,128)(2,1)S(1)} %shard_map.115.refs_0_.refs_2_, bf16[1024,256]{1,0:T(8,128)(2,1)S(1)} %shard_map.111.refs_0_.refs_1_, bf16[1024,256]{1,0:T(8,128)(2,1)S(1)} %shard_map.114.refs_0_.refs_2_, ...), custom_call_target="tpu_custom_call" | custom-call | flops 1 | bytes 1 | tf_op jit(solution)/shard_map/pallas_call | solution.py:249
  91.4 2.8 %shard_map.117 = (f32[896,1024]{1,0:T(8,128)}, f32[1024]{0:T(1024)}, f32[8,128]{1,0:T(8,128)}) custom-call(f32[8,128]{1,0:T(8,128)S(1)} %get-tuple-element.55.refs_0_, bf16[896,512]{1,0:T(8,128)(2,1)S(1)} %shard_map.95.refs_0_.refs_1_, bf16[128,1024]{1,0:T(8,128)(2,1)S(1)} %shard_map.115.refs_0_.refs_2_, bf16[128,1024]{1,0:T(8,128)(2,1)S(1)} %shard_map.112.refs_0_.refs_3_, ...), custom_call_target="tpu_custom_call" | custom-call | flops 1 | bytes 1 | tf_op jit(solution)/shard_map/pallas_call | solution.py:249
  (57 shorter events, 11.7 us)
Async XLA Ops:
  0.6 6.7 %copy-start = (bf16[896,1024]{1,0:T(8,128)(2,1)S(1)}, bf16[896,1024]{1,0:T(8,128)(2,1)}, u32[]{:S(2)}) copy-start(bf16[896,1024]{1,0:T(8,128)(2,1)} %refs_2_.2) | copy-start | bytes 5505028
  0.6 13.7 %collective-permute-start.2 = (bf16[1024,896]{1,0:T(8,128)(2,1)}, bf16[1024,896]{1,0:T(8,128)(2,1)}, u32[]{:S(2)}, u32[]{:S(2)}) collective-permute-start(bf16[1024,896]{1,0:T(8,128)(2,1)} %refs_1_.1), channel_id=1, source_target_pairs={{0,1},{1,0},{2,3},{3,2},{4,5},{5,4},{6,7},{7,6},{8,9},{9,8},{10,11... | collective-permute-start | bytes 5505032 | tf_op jit(solution)/shard_map/decoder2/ppermute | solution.py:262
  7.2 1.9 %collective-permute-start = (bf16[128,1024]{1,0:T(8,128)(2,1)S(1)}, bf16[128,1024]{1,0:T(8,128)(2,1)S(1)}, u32[]{:S(2)}, u32[]{:S(2)}) collective-permute-start(bf16[128,1024]{1,0:T(8,128)(2,1)S(1)} %get-tuple-element.33), channel_id=1, source_target_pairs={{0,1},{1,0},{2,3},{3,2},{4,5},{5,4},{6,7},{7,6},{8,9},{9,8},{10,11... | collective-permute-start | bytes 786440 | tf_op jit(solution)/shard_map/got0/ppermute | solution.py:262
  8.6 2.3 %collective-permute-start.1 = (bf16[128,1024]{1,0:T(8,128)(2,1)S(1)}, bf16[128,1024]{1,0:T(8,128)(2,1)S(1)}, u32[]{:S(2)}, u32[]{:S(2)}) collective-permute-start(bf16[128,1024]{1,0:T(8,128)(2,1)S(1)} %get-tuple-element.37), channel_id=1, source_target_pairs={{0,1},{1,0},{2,3},{3,2},{4,5},{5,4},{6,7},{7,6},{8,9},{9,8},{10,11... | collective-permute-start | bytes 786440 | tf_op jit(solution)/shard_map/got1/ppermute | solution.py:262
  9.2 8.0 %collective-permute-start.4 = (bf16[128,1024]{1,0:T(8,128)(2,1)S(1)}, bf16[128,1024]{1,0:T(8,128)(2,1)S(1)}, u32[]{:S(2)}, u32[]{:S(2)}) collective-permute-start(bf16[128,1024]{1,0:T(8,128)(2,1)S(1)} %shard_map.94.refs_0_.refs_4_), channel_id=1, source_target_pairs={{0,2},{2,0},{1,3},{3,1},{4,6},{6,4},{5,7},{7,5},{8,10},{10,8},{9,1... | collective-permute-start | bytes 786440 | tf_op jit(solution)/shard_map/away0/ppermute | solution.py:262
  10.2 3.6 %copy-start.1 = (bf16[1024,896]{1,0:T(8,128)(2,1)S(1)}, bf16[1024,896]{1,0:T(8,128)(2,1)}, u32[]{:S(2)}) copy-start(bf16[1024,896]{1,0:T(8,128)(2,1)} %refs_1_.1) | copy-start | bytes 5505028
  10.9 11.8 %collective-permute-start.5 = (bf16[128,1024]{1,0:T(8,128)(2,1)S(1)}, bf16[128,1024]{1,0:T(8,128)(2,1)S(1)}, u32[]{:S(2)}, u32[]{:S(2)}) collective-permute-start(bf16[128,1024]{1,0:T(8,128)(2,1)S(1)} %shard_map.98.refs_0_.refs_2_), channel_id=1, source_target_pairs={{0,2},{2,0},{1,3},{3,1},{4,6},{6,4},{5,7},{7,5},{8,10},{10,8},{9,1... | collective-permute-start | bytes 786440 | tf_op jit(solution)/shard_map/away1/ppermute | solution.py:262
  13.0 4.1 %copy-start.2 = (f32[1024]{0:T(1024)S(1)}, f32[1024]{0:T(1024)}, u32[]{:S(2)}) copy-start(f32[1024]{0:T(1024)} %refs_4_.1) | copy-start | bytes 12292
  13.1 3.4 %collective-permute-start.3 = (f32[8,896]{1,0:T(8,128)S(1)}, f32[8,896]{1,0:T(8,128)S(1)}, u32[]{:S(2)}, u32[]{:S(2)}) collective-permute-start(f32[8,896]{1,0:T(8,128)S(1)} %get-tuple-element.40), channel_id=1, source_target_pairs={{0,1},{1,0},{2,3},{3,2},{4,5},{5,4},{6,7},{7,6},{8,9},{9,8},{10,11... | collective-permute-start | bytes 86024 | tf_op jit(solution)/shard_map/base2/ppermute | solution.py:262
  18.0 12.4 %collective-permute-start.7 = (bf16[128,896]{1,0:T(8,128)(2,1)S(1)}, bf16[128,896]{1,0:T(8,128)(2,1)S(1)}, u32[]{:S(2)}, u32[]{:S(2)}) collective-permute-start(bf16[128,896]{1,0:T(8,128)(2,1)S(1)} %get-tuple-element.46), channel_id=1, source_target_pairs={{0,24},{8,16},{16,8},{24,0},{1,25},{9,17},{17,9},{25,1},{2,26},{10... | collective-permute-start | bytes 688136 | tf_op jit(solution)/shard_map/g3/ppermute | solution.py:267
  19.1 11.3 %collective-permute-start.6 = (bf16[128,896]{1,0:T(8,128)(2,1)S(1)}, bf16[128,896]{1,0:T(8,128)(2,1)S(1)}, u32[]{:S(2)}, u32[]{:S(2)}) collective-permute-start(bf16[128,896]{1,0:T(8,128)(2,1)S(1)} %get-tuple-element.43.refs_0_), channel_id=1, source_target_pairs={{0,16},{8,24},{16,0},{24,8},{1,17},{9,25},{17,1},{25,9},{2,18},{10... | collective-permute-start | bytes 688136 | tf_op jit(solution)/shard_map/g2/ppermute | solution.py:267
  23.6 7.8 %collective-permute-start.8 = (bf16[128,896]{1,0:T(8,128)(2,1)S(1)}, bf16[128,896]{1,0:T(8,128)(2,1)S(1)}, u32[]{:S(2)}, u32[]{:S(2)}) collective-permute-start(bf16[128,896]{1,0:T(8,128)(2,1)S(1)} %get-tuple-element.47), channel_id=1, source_target_pairs={{0,8},{8,0},{16,24},{24,16},{1,9},{9,1},{17,25},{25,17},{2,10},{10... | collective-permute-start | bytes 688136 | tf_op jit(solution)/shard_map/g1/ppermute | solution.py:267
  65.2 5.2 %collective-permute-start.9 = (bf16[128,896]{1,0:T(8,128)(2,1)S(1)}, bf16[128,896]{1,0:T(8,128)(2,1)S(1)}, u32[]{:S(2)}, u32[]{:S(2)}) collective-permute-start(bf16[128,896]{1,0:T(8,128)(2,1)S(1)} %bitcast.5), channel_id=1, source_target_pairs={{0,8},{8,0},{16,24},{24,16},{1,9},{9,1},{17,25},{25,17},{2,10},{10... | collective-permute-start | bytes 688136 | tf_op jit(solution)/shard_map/e1/ppermute | solution.py:267
  67.0 7.9 %collective-permute-start.11 = (bf16[128,896]{1,0:T(8,128)(2,1)S(1)}, bf16[128,896]{1,0:T(8,128)(2,1)S(1)}, u32[]{:S(2)}, u32[]{:S(2)}) collective-permute-start(bf16[128,896]{1,0:T(8,128)(2,1)S(1)} %bitcast.6), channel_id=1, source_target_pairs={{0,24},{8,16},{16,8},{24,0},{1,25},{9,17},{17,9},{25,1},{2,26},{10... | collective-permute-start | bytes 688136 | tf_op jit(solution)/shard_map/e3/ppermute | solution.py:267
  68.8 7.3 %collective-permute-start.10 = (bf16[128,896]{1,0:T(8,128)(2,1)S(1)}, bf16[128,896]{1,0:T(8,128)(2,1)S(1)}, u32[]{:S(2)}, u32[]{:S(2)}) collective-permute-start(bf16[128,896]{1,0:T(8,128)(2,1)S(1)} %bitcast.7), channel_id=1, source_target_pairs={{0,16},{8,24},{16,0},{24,8},{1,17},{9,25},{17,1},{25,9},{2,18},{10... | collective-permute-start | bytes 688136 | tf_op jit(solution)/shard_map/e2/ppermute | solution.py:267
  71.1 11.9 %collective-permute-start.13 = (bf16[64,1024]{1,0:T(8,128)(2,1)S(1)}, bf16[64,1024]{1,0:T(8,128)(2,1)S(1)}, u32[]{:S(2)}, u32[]{:S(2)}) collective-permute-start(bf16[64,1024]{1,0:T(8,128)(2,1)S(1)} %get-tuple-element.50.refs_3_), channel_id=1, source_target_pairs={{0,2},{2,0},{1,3},{3,1},{4,6},{6,4},{5,7},{7,5},{8,10},{10,8},{9,1... | collective-permute-start | bytes 393224 | tf_op jit(solution)/shard_map/back1/ppermute | solution.py:262
  71.7 12.6 %collective-permute-start.12 = (bf16[64,1024]{1,0:T(8,128)(2,1)S(1)}, bf16[64,1024]{1,0:T(8,128)(2,1)S(1)}, u32[]{:S(2)}, u32[]{:S(2)}) collective-permute-start(bf16[64,1024]{1,0:T(8,128)(2,1)S(1)} %get-tuple-element.49.refs_0_.refs_2_), channel_id=1, source_target_pairs={{0,2},{2,0},{1,3},{3,1},{4,6},{6,4},{5,7},{7,5},{8,10},{10,8},{9,1... | collective-permute-start | bytes 393224 | tf_op jit(solution)/shard_map/back1/ppermute | solution.py:262
  76.8 10.1 %collective-permute-start.18 = (bf16[128,1024]{1,0:T(8,128)(2,1)S(1)}, bf16[128,1024]{1,0:T(8,128)(2,1)S(1)}, u32[]{:S(2)}, u32[]{:S(2)}) collective-permute-start(bf16[128,1024]{1,0:T(8,128)(2,1)S(1)} %shard_map.110.refs_0_.refs_2_), channel_id=1, source_target_pairs={{0,2},{2,0},{1,3},{3,1},{4,6},{6,4},{5,7},{7,5},{8,10},{10,8},{9,1... | collective-permute-start | bytes 786440 | tf_op jit(solution)/shard_map/back0/ppermute | solution.py:262
  77.4 8.3 %collective-permute-start.14 = (bf16[64,1920]{1,0:T(8,128)(2,1)S(1)}, bf16[64,1920]{1,0:T(8,128)(2,1)S(1)}, u32[]{:S(2)}, u32[]{:S(2)}) collective-permute-start(bf16[64,1920]{1,0:T(8,128)(2,1)S(1)} %get-tuple-element.51), channel_id=1, source_target_pairs={{0,1},{1,0},{2,3},{3,2},{4,5},{5,4},{6,7},{7,6},{8,9},{9,8},{10,11... | collective-permute-start | bytes 737288 | tf_op jit(solution)/shard_map/moved/ppermute | solution.py:262
  82.9 2.9 %collective-permute-start.15 = (bf16[64,1920]{1,0:T(8,128)(2,1)S(1)}, bf16[64,1920]{1,0:T(8,128)(2,1)S(1)}, u32[]{:S(2)}, u32[]{:S(2)}) collective-permute-start(bf16[64,1920]{1,0:T(8,128)(2,1)S(1)} %get-tuple-element.52), channel_id=1, source_target_pairs={{0,1},{1,0},{2,3},{3,2},{4,5},{5,4},{6,7},{7,6},{8,9},{9,8},{10,11... | collective-permute-start | bytes 737288 | tf_op jit(solution)/shard_map/moved/ppermute | solution.py:262
  83.0 2.8 %collective-permute-start.16 = (bf16[64,1920]{1,0:T(8,128)(2,1)S(1)}, bf16[64,1920]{1,0:T(8,128)(2,1)S(1)}, u32[]{:S(2)}, u32[]{:S(2)}) collective-permute-start(bf16[64,1920]{1,0:T(8,128)(2,1)S(1)} %get-tuple-element.53), channel_id=1, source_target_pairs={{0,1},{1,0},{2,3},{3,2},{4,5},{5,4},{6,7},{7,6},{8,9},{9,8},{10,11... | collective-permute-start | bytes 737288 | tf_op jit(solution)/shard_map/moved/ppermute | solution.py:262
  84.2 2.5 %collective-permute-start.17 = (bf16[64,1920]{1,0:T(8,128)(2,1)S(1)}, bf16[64,1920]{1,0:T(8,128)(2,1)S(1)}, u32[]{:S(2)}, u32[]{:S(2)}) collective-permute-start(bf16[64,1920]{1,0:T(8,128)(2,1)S(1)} %get-tuple-element.54), channel_id=1, source_target_pairs={{0,1},{1,0},{2,3},{3,2},{4,5},{5,4},{6,7},{7,6},{8,9},{9,8},{10,11... | collective-permute-start | bytes 737288 | tf_op jit(solution)/shard_map/moved/ppermute | solution.py:262
  85.8 5.7 %collective-permute-start.20 = (bf16[128,1024]{1,0:T(8,128)(2,1)S(1)}, bf16[128,1024]{1,0:T(8,128)(2,1)S(1)}, u32[]{:S(2)}, u32[]{:S(2)}) collective-permute-start(bf16[128,1024]{1,0:T(8,128)(2,1)S(1)} %shard_map.112.refs_0_.refs_3_), channel_id=1, source_target_pairs={{0,1},{1,0},{2,3},{3,2},{4,5},{5,4},{6,7},{7,6},{8,9},{9,8},{10,11... | collective-permute-start | bytes 786440 | tf_op jit(solution)/shard_map/pre1o/ppermute | solution.py:262
  87.1 4.3 %collective-permute-start.19 = (bf16[128,1024]{1,0:T(8,128)(2,1)S(1)}, bf16[128,1024]{1,0:T(8,128)(2,1)S(1)}, u32[]{:S(2)}, u32[]{:S(2)}) collective-permute-start(bf16[128,1024]{1,0:T(8,128)(2,1)S(1)} %shard_map.115.refs_0_.refs_2_), channel_id=1, source_target_pairs={{0,1},{1,0},{2,3},{3,2},{4,5},{5,4},{6,7},{7,6},{8,9},{9,8},{10,11... | collective-permute-start | bytes 786440 | tf_op jit(solution)/shard_map/pre0o/ppermute | solution.py:262
  (2 other events, 5.3 us)

commit v4 on v3

--- a/solution.py
+++ b/solution.py
@@ -11,7 +11,7 @@
 CHUNK = 2 * Q
 LAT = ("z", "y", "xh")
 WID = ("xl", "c")
-FAR = ("z", "xh")
+FAR = ("xh", "z")
 PEERS = 16
 ROWS = CHUNK // PEERS
 FIRST_LIMIT = 52

time: 94.6 us -> 92.4 us (0.977)
  blocking collectives: 33.2 us -> 31.4 us
    all_to_all x1, blocking collectives: 19.8 us -> 17.9 us  [shards(): pieces = lax.all_to_all(total.reshape(PEERS, ROWS, d), FAR, 0, 0)]
where the time goes in v4:
time: 92.4 us; the launch traced here: 92.2 us
  blocking collectives  31.4 us (34%)
  starting transfers between devices  23.9 us (26%)
  Pallas kernels  19.3 us (21%)
  waiting for transfers between devices  16.4 us (18%)
  between operations  1.11 us (1%)
    ppermute x15, starting transfers between devices, swap(): return lax.ppermute(x, axis, SWAP)  18.3 us
    all_to_all x1, blocking collectives, shards(): pieces = lax.all_to_all(total.reshape(PEERS, ROWS, d), FAR, 0, 0)  17.9 us
    all_to_all x1, blocking collectives, shards(): e0 = lax.all_to_all(copies, FAR, 0, 0).reshape(CHUNK, d)  13.5 us
    ppermute x6, waiting for transfers between devices, partner(): return lax.ppermute(x, 'y', [(i, i ^ r) for i in range(4)])  11.5 us
    pallas_call x22, Pallas kernels, call(): pl.pallas_call(body, out_shape=[jax.ShapeDtypeStruct(s, t) for s, t in ou...  10.6 us
    pallas_call x2, Pallas kernels, product(): pl.pallas_call(kernel, in_specs=[ANY] * skip + [VMEM] * (wide + count), o...  5.59 us
    ppermute x6, starting transfers between devices, partner(): return lax.ppermute(x, 'y', [(i, i ^ r) for i in range(4)])  5.57 us
    ppermute x15, waiting for transfers between devices, swap(): return lax.ppermute(x, axis, SWAP)  4.91 us
  transfers between devices with their start and end apart: 21, of which 8 were waited for; matrix products, arithmetic and copies ran while one was open for 0% of the time, Pallas kernels for 17%

profile of v4, /device:TPU:1, one launch (start us, length us, event | category | flops | bytes accessed | tf_op | source)
XLA Modules:
  0.0 92.2 jit_solution(9414273004824539344)
XLA Ops:
  0.6 3.3 %collective-permute-start.2 = (bf16[1024,896]{1,0:T(8,128)(2,1)}, bf16[1024,896]{1,0:T(8,128)(2,1)}, u32[]{:S(2)}, u32[]{:S(2)}) collective-permute-start(bf16[1024,896]{1,0:T(8,128)(2,1)} %refs_1_.1), channel_id=1, source_target_pairs={{0,1},{1,0},{2,3},{3,2},{4,5},{5,4},{6,7},{7,6},{8,9},{9,8},{10,11... | collective-permute-start | bytes 5505032 | tf_op jit(solution)/shard_map/decoder2/ppermute | solution.py:262
  4.0 3.2 %shard_map.93 = (bf16[128,1024]{1,0:T(8,128)(2,1)S(1)}, bf16[128,1024]{1,0:T(8,128)(2,1)S(1)}, bf16[8,64,896]{2,1,0:T(8,128)(2,1)S(1)}) custom-call(s32[11]{0:T(128)S(1)} %compare_select_fusion.1.ids_ref.refs_1_.refs_0_, bf16[8,64,896]{2,1,0:T(8,128)(2,1)} %bitcast.12, bf16[896,1024]{1,0:T(8,128)(2,1)} %refs_2_.2), custom_call_target="tpu_custom_call" | custom-call | flops 1 | bytes 1 | tf_op jit(solution)/shard_map/pallas_call | solution.py:69
  7.3 1.2 %shard_map.97 = (bf16[128,1024]{1,0:T(8,128)(2,1)S(1)}, bf16[128,1024]{1,0:T(8,128)(2,1)S(1)}) custom-call(s32[11]{0:T(128)S(1)} %compare_select_fusion.1.ids_ref.refs_1_.refs_0_, bf16[8,64,896]{2,1,0:T(8,128)(2,1)S(1)} %get-tuple-element.34.refs_2_.refs_1_, bf16[896,1024]{1,0:T(8,128)(2,1)S(1)} %copy-done), custom_call_target="tpu_custom_call" | custom-call | flops 1 | bytes 1 | tf_op jit(solution)/shard_map/pallas_call | solution.py:37
  10.9 1.5 %collective-permute-start.5 = (bf16[128,1024]{1,0:T(8,128)(2,1)S(1)}, bf16[128,1024]{1,0:T(8,128)(2,1)S(1)}, u32[]{:S(2)}, u32[]{:S(2)}) collective-permute-start(bf16[128,1024]{1,0:T(8,128)(2,1)S(1)} %shard_map.98.refs_0_.refs_2_), channel_id=1, source_target_pairs={{0,2},{2,0},{1,3},{3,1},{4,6},{6,4},{5,7},{7,5},{8,10},{10,8},{9,1... | collective-permute-start | bytes 786440 | tf_op jit(solution)/shard_map/away1/ppermute | solution.py:262
  14.4 2.1 %shard_map.100 = (bf16[896,1024]{1,0:T(8,128)(2,1)S(1)}, bf16[1024,896]{1,0:T(8,128)(2,1)S(1)}) custom-call(bf16[128,1024]{1,0:T(8,128)(2,1)S(1)} %shard_map.98.refs_0_.refs_2_, bf16[1024,896]{1,0:T(8,128)(2,1)} %collective-permute-done.2.refs_1_), custom_call_target="tpu_custom_call" | custom-call | flops 1 | bytes 1 | tf_op jit(solution)/shard_map/pallas_call | solution.py:37
  18.0 1.1 %collective-permute-start.7 = (bf16[128,896]{1,0:T(8,128)(2,1)S(1)}, bf16[128,896]{1,0:T(8,128)(2,1)S(1)}, u32[]{:S(2)}, u32[]{:S(2)}) collective-permute-start(bf16[128,896]{1,0:T(8,128)(2,1)S(1)} %get-tuple-element.46), channel_id=1, source_target_pairs={{0,24},{8,16},{16,8},{24,0},{1,25},{9,17},{17,9},{25,1},{2,26},{10... | collective-permute-start | bytes 688136 | tf_op jit(solution)/shard_map/g3/ppermute | solution.py:267
  19.4 3.3 %collective-permute-done.5.refs_3_ = bf16[128,1024]{1,0:T(8,128)(2,1)S(1)} collective-permute-done((bf16[128,1024]{1,0:T(8,128)(2,1)S(1)}, bf16[128,1024]{1,0:T(8,128)(2,1)S(1)}, u32[]{:S(2)}, u32[]{:S(2)}) %collective-permute-start.5) | collective-permute-done | bytes 262176 | tf_op jit(solution)/shard_map/away1/ppermute | solution.py:262
  23.7 6.7 %collective-permute-done.7.refs_2_ = bf16[128,896]{1,0:T(8,128)(2,1)S(1)} collective-permute-done((bf16[128,896]{1,0:T(8,128)(2,1)S(1)}, bf16[128,896]{1,0:T(8,128)(2,1)S(1)}, u32[]{:S(2)}, u32[]{:S(2)}) %collective-permute-start.7) | collective-permute-done | bytes 229408 | tf_op jit(solution)/shard_map/g3/ppermute | solution.py:267
  30.5 0.9 %collective-permute-done.8.refs_1_ = bf16[128,896]{1,0:T(8,128)(2,1)S(1)} collective-permute-done((bf16[128,896]{1,0:T(8,128)(2,1)S(1)}, bf16[128,896]{1,0:T(8,128)(2,1)S(1)}, u32[]{:S(2)}, u32[]{:S(2)}) %collective-permute-start.8) | collective-permute-done | bytes 229408 | tf_op jit(solution)/shard_map/g1/ppermute | solution.py:267
  31.4 17.9 %all_to_all.10.refs_1_ = bf16[16,8,896]{2,1,0:T(8,128)(2,1)S(1)} all-to-all(bf16[16,8,896]{2,1,0:T(8,128)(2,1)S(1)} %bitcast.11), channel_id=1, replica_groups=mesh['z'=8,'y'=4,'xh'=2,'xl'=2,'c'=2] {'xh','z'}, dimensions={0} | all-to-all | bytes 458752 | tf_op jit(solution)/shard_map/all_to_all | solution.py:332
  49.9 13.5 %all_to_all.11 = bf16[16,8,896]{2,1,0:T(8,128)(2,1)S(1)} all-to-all(bf16[16,8,896]{2,1,0:T(8,128)(2,1)S(1)} %shard_map.108), channel_id=1, replica_groups=mesh['z'=8,'y'=4,'xh'=2,'xl'=2,'c'=2] {'xh','z'}, dimensions={0} | all-to-all | bytes 458752 | tf_op jit(solution)/shard_map/all_to_all | solution.py:334
  63.4 1.4 %collective-permute-start.9 = (bf16[128,896]{1,0:T(8,128)(2,1)S(1)}, bf16[128,896]{1,0:T(8,128)(2,1)S(1)}, u32[]{:S(2)}, u32[]{:S(2)}) collective-permute-start(bf16[128,896]{1,0:T(8,128)(2,1)S(1)} %bitcast.5), channel_id=1, source_target_pairs={{0,8},{8,0},{16,24},{24,16},{1,9},{9,1},{17,25},{25,17},{2,10},{10... | collective-permute-start | bytes 688136 | tf_op jit(solution)/shard_map/e1/ppermute | solution.py:267
  64.8 1.9 %collective-permute-start.11 = (bf16[128,896]{1,0:T(8,128)(2,1)S(1)}, bf16[128,896]{1,0:T(8,128)(2,1)S(1)}, u32[]{:S(2)}, u32[]{:S(2)}) collective-permute-start(bf16[128,896]{1,0:T(8,128)(2,1)S(1)} %bitcast.6), channel_id=1, source_target_pairs={{0,24},{8,16},{16,8},{24,0},{1,25},{9,17},{17,9},{25,1},{2,26},{10... | collective-permute-start | bytes 688136 | tf_op jit(solution)/shard_map/e3/ppermute | solution.py:267
  67.5 0.8 collective-permute-done.9.refs_0_.refs_3_.refs_5_
  69.6 1.1 %collective-permute-start.12 = (bf16[64,1024]{1,0:T(8,128)(2,1)S(1)}, bf16[64,1024]{1,0:T(8,128)(2,1)S(1)}, u32[]{:S(2)}, u32[]{:S(2)}) collective-permute-start(bf16[64,1024]{1,0:T(8,128)(2,1)S(1)} %get-tuple-element.49.refs_0_.refs_2_), channel_id=1, source_target_pairs={{0,2},{2,0},{1,3},{3,1},{4,6},{6,4},{5,7},{7,5},{8,10},{10,8},{9,1... | collective-permute-start | bytes 393224 | tf_op jit(solution)/shard_map/back1/ppermute | solution.py:262
  70.8 1.3 %collective-permute-done.11.refs_2_.refs_4_ = bf16[128,896]{1,0:T(8,128)(2,1)S(1)} collective-permute-done((bf16[128,896]{1,0:T(8,128)(2,1)S(1)}, bf16[128,896]{1,0:T(8,128)(2,1)S(1)}, u32[]{:S(2)}, u32[]{:S(2)}) %collective-permute-start.11) | collective-permute-done | bytes 229408 | tf_op jit(solution)/shard_map/e3/ppermute | solution.py:267
  72.1 1.7 %collective-permute-done.10.refs_1_.refs_3_ = bf16[128,896]{1,0:T(8,128)(2,1)S(1)} collective-permute-done((bf16[128,896]{1,0:T(8,128)(2,1)S(1)}, bf16[128,896]{1,0:T(8,128)(2,1)S(1)}, u32[]{:S(2)}, u32[]{:S(2)}) %collective-permute-start.10) | collective-permute-done | bytes 229408 | tf_op jit(solution)/shard_map/e2/ppermute | solution.py:267
  75.2 5.6 %collective-permute-start.14 = (bf16[64,1920]{1,0:T(8,128)(2,1)S(1)}, bf16[64,1920]{1,0:T(8,128)(2,1)S(1)}, u32[]{:S(2)}, u32[]{:S(2)}) collective-permute-start(bf16[64,1920]{1,0:T(8,128)(2,1)S(1)} %get-tuple-element.51), channel_id=1, source_target_pairs={{0,1},{1,0},{2,3},{3,2},{4,5},{5,4},{6,7},{7,6},{8,9},{9,8},{10,11... | collective-permute-start | bytes 737288 | tf_op jit(solution)/shard_map/moved/ppermute | solution.py:262
  81.0 1.0 %collective-permute-start.16 = (bf16[64,1920]{1,0:T(8,128)(2,1)S(1)}, bf16[64,1920]{1,0:T(8,128)(2,1)S(1)}, u32[]{:S(2)}, u32[]{:S(2)}) collective-permute-start(bf16[64,1920]{1,0:T(8,128)(2,1)S(1)} %get-tuple-element.53), channel_id=1, source_target_pairs={{0,1},{1,0},{2,3},{3,2},{4,5},{5,4},{6,7},{7,6},{8,9},{9,8},{10,11... | collective-permute-start | bytes 737288 | tf_op jit(solution)/shard_map/moved/ppermute | solution.py:262
  82.0 1.4 %collective-permute-start.17 = (bf16[64,1920]{1,0:T(8,128)(2,1)S(1)}, bf16[64,1920]{1,0:T(8,128)(2,1)S(1)}, u32[]{:S(2)}, u32[]{:S(2)}) collective-permute-start(bf16[64,1920]{1,0:T(8,128)(2,1)S(1)} %get-tuple-element.54), channel_id=1, source_target_pairs={{0,1},{1,0},{2,3},{3,2},{4,5},{5,4},{6,7},{7,6},{8,9},{9,8},{10,11... | collective-permute-start | bytes 737288 | tf_op jit(solution)/shard_map/moved/ppermute | solution.py:262
  83.6 0.9 collective-permute-done.17.refs_4_.refs_10_
  84.8 1.6 %collective-permute-start.19 = (bf16[128,1024]{1,0:T(8,128)(2,1)S(1)}, bf16[128,1024]{1,0:T(8,128)(2,1)S(1)}, u32[]{:S(2)}, u32[]{:S(2)}) collective-permute-start(bf16[128,1024]{1,0:T(8,128)(2,1)S(1)} %shard_map.115.refs_0_.refs_2_), channel_id=1, source_target_pairs={{0,1},{1,0},{2,3},{3,2},{4,5},{5,4},{6,7},{7,6},{8,9},{9,8},{10,11... | collective-permute-start | bytes 786440 | tf_op jit(solution)/shard_map/pre0o/ppermute | solution.py:262
  86.4 2.8 %shard_map.116 = (f32[1024,896]{1,0:T(8,128)}, f32[896]{0:T(1024)}, f32[8,128]{1,0:T(8,128)S(1)}) custom-call(bf16[128,1024]{1,0:T(8,128)(2,1)S(1)} %shard_map.115.refs_0_.refs_2_, bf16[1024,256]{1,0:T(8,128)(2,1)S(1)} %shard_map.111.refs_0_.refs_1_, bf16[1024,256]{1,0:T(8,128)(2,1)S(1)} %shard_map.114.refs_0_.refs_2_, ...), custom_call_target="tpu_custom_call" | custom-call | flops 1 | bytes 1 | tf_op jit(solution)/shard_map/pallas_call | solution.py:249
  89.3 2.8 %shard_map.117 = (f32[896,1024]{1,0:T(8,128)}, f32[1024]{0:T(1024)}, f32[8,128]{1,0:T(8,128)}) custom-call(f32[8,128]{1,0:T(8,128)S(1)} %get-tuple-element.55.refs_0_, bf16[896,512]{1,0:T(8,128)(2,1)S(1)} %shard_map.95.refs_0_.refs_1_, bf16[128,1024]{1,0:T(8,128)(2,1)S(1)} %shard_map.115.refs_0_.refs_2_, bf16[128,1024]{1,0:T(8,128)(2,1)S(1)} %shard_map.112.refs_0_.refs_3_, ...), custom_call_target="tpu_custom_call" | custom-call | flops 1 | bytes 1 | tf_op jit(solution)/shard_map/pallas_call | solution.py:249
  (57 shorter events, 11.9 us)
Async XLA Ops:
  0.6 6.7 %copy-start = (bf16[896,1024]{1,0:T(8,128)(2,1)S(1)}, bf16[896,1024]{1,0:T(8,128)(2,1)}, u32[]{:S(2)}) copy-start(bf16[896,1024]{1,0:T(8,128)(2,1)} %refs_2_.2) | copy-start | bytes 5505028
  0.6 13.7 %collective-permute-start.2 = (bf16[1024,896]{1,0:T(8,128)(2,1)}, bf16[1024,896]{1,0:T(8,128)(2,1)}, u32[]{:S(2)}, u32[]{:S(2)}) collective-permute-start(bf16[1024,896]{1,0:T(8,128)(2,1)} %refs_1_.1), channel_id=1, source_target_pairs={{0,1},{1,0},{2,3},{3,2},{4,5},{5,4},{6,7},{7,6},{8,9},{9,8},{10,11... | collective-permute-start | bytes 5505032 | tf_op jit(solution)/shard_map/decoder2/ppermute | solution.py:262
  7.2 1.9 %collective-permute-start = (bf16[128,1024]{1,0:T(8,128)(2,1)S(1)}, bf16[128,1024]{1,0:T(8,128)(2,1)S(1)}, u32[]{:S(2)}, u32[]{:S(2)}) collective-permute-start(bf16[128,1024]{1,0:T(8,128)(2,1)S(1)} %get-tuple-element.33), channel_id=1, source_target_pairs={{0,1},{1,0},{2,3},{3,2},{4,5},{5,4},{6,7},{7,6},{8,9},{9,8},{10,11... | collective-permute-start | bytes 786440 | tf_op jit(solution)/shard_map/got0/ppermute | solution.py:262
  8.6 2.3 %collective-permute-start.1 = (bf16[128,1024]{1,0:T(8,128)(2,1)S(1)}, bf16[128,1024]{1,0:T(8,128)(2,1)S(1)}, u32[]{:S(2)}, u32[]{:S(2)}) collective-permute-start(bf16[128,1024]{1,0:T(8,128)(2,1)S(1)} %get-tuple-element.37), channel_id=1, source_target_pairs={{0,1},{1,0},{2,3},{3,2},{4,5},{5,4},{6,7},{7,6},{8,9},{9,8},{10,11... | collective-permute-start | bytes 786440 | tf_op jit(solution)/shard_map/got1/ppermute | solution.py:262
  9.2 8.0 %collective-permute-start.4 = (bf16[128,1024]{1,0:T(8,128)(2,1)S(1)}, bf16[128,1024]{1,0:T(8,128)(2,1)S(1)}, u32[]{:S(2)}, u32[]{:S(2)}) collective-permute-start(bf16[128,1024]{1,0:T(8,128)(2,1)S(1)} %shard_map.94.refs_0_.refs_4_), channel_id=1, source_target_pairs={{0,2},{2,0},{1,3},{3,1},{4,6},{6,4},{5,7},{7,5},{8,10},{10,8},{9,1... | collective-permute-start | bytes 786440 | tf_op jit(solution)/shard_map/away0/ppermute | solution.py:262
  10.2 3.6 %copy-start.1 = (bf16[1024,896]{1,0:T(8,128)(2,1)S(1)}, bf16[1024,896]{1,0:T(8,128)(2,1)}, u32[]{:S(2)}) copy-start(bf16[1024,896]{1,0:T(8,128)(2,1)} %refs_1_.1) | copy-start | bytes 5505028
  10.9 11.8 %collective-permute-start.5 = (bf16[128,1024]{1,0:T(8,128)(2,1)S(1)}, bf16[128,1024]{1,0:T(8,128)(2,1)S(1)}, u32[]{:S(2)}, u32[]{:S(2)}) collective-permute-start(bf16[128,1024]{1,0:T(8,128)(2,1)S(1)} %shard_map.98.refs_0_.refs_2_), channel_id=1, source_target_pairs={{0,2},{2,0},{1,3},{3,1},{4,6},{6,4},{5,7},{7,5},{8,10},{10,8},{9,1... | collective-permute-start | bytes 786440 | tf_op jit(solution)/shard_map/away1/ppermute | solution.py:262
  13.0 4.1 %copy-start.2 = (f32[1024]{0:T(1024)S(1)}, f32[1024]{0:T(1024)}, u32[]{:S(2)}) copy-start(f32[1024]{0:T(1024)} %refs_4_.1) | copy-start | bytes 12292
  13.1 3.4 %collective-permute-start.3 = (f32[8,896]{1,0:T(8,128)S(1)}, f32[8,896]{1,0:T(8,128)S(1)}, u32[]{:S(2)}, u32[]{:S(2)}) collective-permute-start(f32[8,896]{1,0:T(8,128)S(1)} %get-tuple-element.40), channel_id=1, source_target_pairs={{0,1},{1,0},{2,3},{3,2},{4,5},{5,4},{6,7},{7,6},{8,9},{9,8},{10,11... | collective-permute-start | bytes 86024 | tf_op jit(solution)/shard_map/base2/ppermute | solution.py:262
  18.0 12.4 %collective-permute-start.7 = (bf16[128,896]{1,0:T(8,128)(2,1)S(1)}, bf16[128,896]{1,0:T(8,128)(2,1)S(1)}, u32[]{:S(2)}, u32[]{:S(2)}) collective-permute-start(bf16[128,896]{1,0:T(8,128)(2,1)S(1)} %get-tuple-element.46), channel_id=1, source_target_pairs={{0,24},{8,16},{16,8},{24,0},{1,25},{9,17},{17,9},{25,1},{2,26},{10... | collective-permute-start | bytes 688136 | tf_op jit(solution)/shard_map/g3/ppermute | solution.py:267
  19.1 11.3 %collective-permute-start.6 = (bf16[128,896]{1,0:T(8,128)(2,1)S(1)}, bf16[128,896]{1,0:T(8,128)(2,1)S(1)}, u32[]{:S(2)}, u32[]{:S(2)}) collective-permute-start(bf16[128,896]{1,0:T(8,128)(2,1)S(1)} %get-tuple-element.43.refs_0_), channel_id=1, source_target_pairs={{0,16},{8,24},{16,0},{24,8},{1,17},{9,25},{17,1},{25,9},{2,18},{10... | collective-permute-start | bytes 688136 | tf_op jit(solution)/shard_map/g2/ppermute | solution.py:267
  23.6 7.8 %collective-permute-start.8 = (bf16[128,896]{1,0:T(8,128)(2,1)S(1)}, bf16[128,896]{1,0:T(8,128)(2,1)S(1)}, u32[]{:S(2)}, u32[]{:S(2)}) collective-permute-start(bf16[128,896]{1,0:T(8,128)(2,1)S(1)} %get-tuple-element.47), channel_id=1, source_target_pairs={{0,8},{8,0},{16,24},{24,16},{1,9},{9,1},{17,25},{25,17},{2,10},{10... | collective-permute-start | bytes 688136 | tf_op jit(solution)/shard_map/g1/ppermute | solution.py:267
  63.4 4.9 %collective-permute-start.9 = (bf16[128,896]{1,0:T(8,128)(2,1)S(1)}, bf16[128,896]{1,0:T(8,128)(2,1)S(1)}, u32[]{:S(2)}, u32[]{:S(2)}) collective-permute-start(bf16[128,896]{1,0:T(8,128)(2,1)S(1)} %bitcast.5), channel_id=1, source_target_pairs={{0,8},{8,0},{16,24},{24,16},{1,9},{9,1},{17,25},{25,17},{2,10},{10... | collective-permute-start | bytes 688136 | tf_op jit(solution)/shard_map/e1/ppermute | solution.py:267
  64.8 7.2 %collective-permute-start.11 = (bf16[128,896]{1,0:T(8,128)(2,1)S(1)}, bf16[128,896]{1,0:T(8,128)(2,1)S(1)}, u32[]{:S(2)}, u32[]{:S(2)}) collective-permute-start(bf16[128,896]{1,0:T(8,128)(2,1)S(1)} %bitcast.6), channel_id=1, source_target_pairs={{0,24},{8,16},{16,8},{24,0},{1,25},{9,17},{17,9},{25,1},{2,26},{10... | collective-permute-start | bytes 688136 | tf_op jit(solution)/shard_map/e3/ppermute | solution.py:267
  66.7 7.1 %collective-permute-start.10 = (bf16[128,896]{1,0:T(8,128)(2,1)S(1)}, bf16[128,896]{1,0:T(8,128)(2,1)S(1)}, u32[]{:S(2)}, u32[]{:S(2)}) collective-permute-start(bf16[128,896]{1,0:T(8,128)(2,1)S(1)} %bitcast.7), channel_id=1, source_target_pairs={{0,16},{8,24},{16,0},{24,8},{1,17},{9,25},{17,1},{25,9},{2,18},{10... | collective-permute-start | bytes 688136 | tf_op jit(solution)/shard_map/e2/ppermute | solution.py:267
  69.0 11.9 %collective-permute-start.13 = (bf16[64,1024]{1,0:T(8,128)(2,1)S(1)}, bf16[64,1024]{1,0:T(8,128)(2,1)S(1)}, u32[]{:S(2)}, u32[]{:S(2)}) collective-permute-start(bf16[64,1024]{1,0:T(8,128)(2,1)S(1)} %get-tuple-element.50.refs_3_), channel_id=1, source_target_pairs={{0,2},{2,0},{1,3},{3,1},{4,6},{6,4},{5,7},{7,5},{8,10},{10,8},{9,1... | collective-permute-start | bytes 393224 | tf_op jit(solution)/shard_map/back1/ppermute | solution.py:262
  69.6 12.3 %collective-permute-start.12 = (bf16[64,1024]{1,0:T(8,128)(2,1)S(1)}, bf16[64,1024]{1,0:T(8,128)(2,1)S(1)}, u32[]{:S(2)}, u32[]{:S(2)}) collective-permute-start(bf16[64,1024]{1,0:T(8,128)(2,1)S(1)} %get-tuple-element.49.refs_0_.refs_2_), channel_id=1, source_target_pairs={{0,2},{2,0},{1,3},{3,1},{4,6},{6,4},{5,7},{7,5},{8,10},{10,8},{9,1... | collective-permute-start | bytes 393224 | tf_op jit(solution)/shard_map/back1/ppermute | solution.py:262
  74.5 10.1 %collective-permute-start.18 = (bf16[128,1024]{1,0:T(8,128)(2,1)S(1)}, bf16[128,1024]{1,0:T(8,128)(2,1)S(1)}, u32[]{:S(2)}, u32[]{:S(2)}) collective-permute-start(bf16[128,1024]{1,0:T(8,128)(2,1)S(1)} %shard_map.110.refs_0_.refs_2_), channel_id=1, source_target_pairs={{0,2},{2,0},{1,3},{3,1},{4,6},{6,4},{5,7},{7,5},{8,10},{10,8},{9,1... | collective-permute-start | bytes 786440 | tf_op jit(solution)/shard_map/back0/ppermute | solution.py:262
  75.2 8.2 %collective-permute-start.14 = (bf16[64,1920]{1,0:T(8,128)(2,1)S(1)}, bf16[64,1920]{1,0:T(8,128)(2,1)S(1)}, u32[]{:S(2)}, u32[]{:S(2)}) collective-permute-start(bf16[64,1920]{1,0:T(8,128)(2,1)S(1)} %get-tuple-element.51), channel_id=1, source_target_pairs={{0,1},{1,0},{2,3},{3,2},{4,5},{5,4},{6,7},{7,6},{8,9},{9,8},{10,11... | collective-permute-start | bytes 737288 | tf_op jit(solution)/shard_map/moved/ppermute | solution.py:262
  80.9 2.7 %collective-permute-start.15 = (bf16[64,1920]{1,0:T(8,128)(2,1)S(1)}, bf16[64,1920]{1,0:T(8,128)(2,1)S(1)}, u32[]{:S(2)}, u32[]{:S(2)}) collective-permute-start(bf16[64,1920]{1,0:T(8,128)(2,1)S(1)} %get-tuple-element.52), channel_id=1, source_target_pairs={{0,1},{1,0},{2,3},{3,2},{4,5},{5,4},{6,7},{7,6},{8,9},{9,8},{10,11... | collective-permute-start | bytes 737288 | tf_op jit(solution)/shard_map/moved/ppermute | solution.py:262
  81.0 2.6 %collective-permute-start.16 = (bf16[64,1920]{1,0:T(8,128)(2,1)S(1)}, bf16[64,1920]{1,0:T(8,128)(2,1)S(1)}, u32[]{:S(2)}, u32[]{:S(2)}) collective-permute-start(bf16[64,1920]{1,0:T(8,128)(2,1)S(1)} %get-tuple-element.53), channel_id=1, source_target_pairs={{0,1},{1,0},{2,3},{3,2},{4,5},{5,4},{6,7},{7,6},{8,9},{9,8},{10,11... | collective-permute-start | bytes 737288 | tf_op jit(solution)/shard_map/moved/ppermute | solution.py:262
  82.0 2.5 %collective-permute-start.17 = (bf16[64,1920]{1,0:T(8,128)(2,1)S(1)}, bf16[64,1920]{1,0:T(8,128)(2,1)S(1)}, u32[]{:S(2)}, u32[]{:S(2)}) collective-permute-start(bf16[64,1920]{1,0:T(8,128)(2,1)S(1)} %get-tuple-element.54), channel_id=1, source_target_pairs={{0,1},{1,0},{2,3},{3,2},{4,5},{5,4},{6,7},{7,6},{8,9},{9,8},{10,11... | collective-permute-start | bytes 737288 | tf_op jit(solution)/shard_map/moved/ppermute | solution.py:262
  83.5 5.8 %collective-permute-start.20 = (bf16[128,1024]{1,0:T(8,128)(2,1)S(1)}, bf16[128,1024]{1,0:T(8,128)(2,1)S(1)}, u32[]{:S(2)}, u32[]{:S(2)}) collective-permute-start(bf16[128,1024]{1,0:T(8,128)(2,1)S(1)} %shard_map.112.refs_0_.refs_3_), channel_id=1, source_target_pairs={{0,1},{1,0},{2,3},{3,2},{4,5},{5,4},{6,7},{7,6},{8,9},{9,8},{10,11... | collective-permute-start | bytes 786440 | tf_op jit(solution)/shard_map/pre1o/ppermute | solution.py:262
  84.8 4.4 %collective-permute-start.19 = (bf16[128,1024]{1,0:T(8,128)(2,1)S(1)}, bf16[128,1024]{1,0:T(8,128)(2,1)S(1)}, u32[]{:S(2)}, u32[]{:S(2)}) collective-permute-start(bf16[128,1024]{1,0:T(8,128)(2,1)S(1)} %shard_map.115.refs_0_.refs_2_), channel_id=1, source_target_pairs={{0,1},{1,0},{2,3},{3,2},{4,5},{5,4},{6,7},{7,6},{8,9},{9,8},{10,11... | collective-permute-start | bytes 786440 | tf_op jit(solution)/shard_map/pre0o/ppermute | solution.py:262
  (2 other events, 5.3 us)

commit v5 on v4

--- a/solution.py
+++ b/solution.py
@@ -9,9 +9,9 @@
 MB_TOK = 256
 Q = 64
 CHUNK = 2 * Q
-LAT = ("z", "y", "xh")
+LAT = ("za", "zb", "zc", "y", "xh")
 WID = ("xl", "c")
-FAR = ("xh", "z")
+FAR = ("xh", "za", "zc", "zb")
 PEERS = 16
 ROWS = CHUNK // PEERS
 FIRST_LIMIT = 52
@@ -352,7 +352,7 @@
 
 
 def solution(mesh):
-    fine = Mesh(mesh.devices.reshape(8, 4, 2, 2, 2), LAT + WID)
+    fine = Mesh(mesh.devices.reshape(2, 2, 2, 4, 2, 2, 2), LAT + WID)
     in_specs = (P(None, None, WID), P(WID, LAT), P(LAT, WID), P(LAT), P(WID), P(None, None, LAT))
     out_specs = (P(WID, LAT), P(LAT, WID), P(LAT), P(WID))
     return jax.shard_map(shards, mesh=fine, in_specs=in_specs, out_specs=out_specs, check_vma=False)

time: 92.4 us -> 92.8 us (level)
  no operation moved by 1% of the time
where the time goes in v5:
time: 92.8 us; the launch traced here: 92.6 us
  blocking collectives  31.2 us (34%)
  starting transfers between devices  24.7 us (27%)
  Pallas kernels  19.3 us (21%)
  waiting for transfers between devices  16.1 us (17%)
  between operations  1.1 us (1%)
    ppermute x15, starting transfers between devices, swap(): return lax.ppermute(x, axis, SWAP)  19.1 us
    all_to_all x1, blocking collectives, shards(): pieces = lax.all_to_all(total.reshape(PEERS, ROWS, d), FAR, 0, 0)  18 us
    all_to_all x1, blocking collectives, shards(): e0 = lax.all_to_all(copies, FAR, 0, 0).reshape(CHUNK, d)  13.3 us
    ppermute x6, waiting for transfers between devices, partner(): return lax.ppermute(x, 'y', [(i, i ^ r) for i in range(4)])  11.2 us
    pallas_call x22, Pallas kernels, call(): pl.pallas_call(body, out_shape=[jax.ShapeDtypeStruct(s, t) for s, t in ou...  10.6 us
    ppermute x6, starting transfers between devices, partner(): return lax.ppermute(x, 'y', [(i, i ^ r) for i in range(4)])  5.67 us
    pallas_call x2, Pallas kernels, product(): pl.pallas_call(kernel, in_specs=[ANY] * skip + [VMEM] * (wide + count), o...  5.59 us
    ppermute x15, waiting for transfers between devices, swap(): return lax.ppermute(x, axis, SWAP)  4.92 us
  transfers between devices with their start and end apart: 21, of which 8 were waited for; matrix products, arithmetic and copies ran while one was open for 0% of the time, Pallas kernels for 17%

profile of v5, /device:TPU:1, one launch (start us, length us, event | category | flops | bytes accessed | tf_op | source)
XLA Modules:
  0.0 92.6 jit_solution(13845339445488927787)
XLA Ops:
  0.6 3.3 %collective-permute-start.2 = (bf16[1024,896]{1,0:T(8,128)(2,1)}, bf16[1024,896]{1,0:T(8,128)(2,1)}, u32[]{:S(2)}, u32[]{:S(2)}) collective-permute-start(bf16[1024,896]{1,0:T(8,128)(2,1)} %refs_1_.1), channel_id=1, source_target_pairs={{0,1},{1,0},{2,3},{3,2},{4,5},{5,4},{6,7},{7,6},{8,9},{9,8},{10,11... | collective-permute-start | bytes 5505032 | tf_op jit(solution)/shard_map/decoder2/ppermute | solution.py:262
  4.0 3.2 %shard_map.93 = (bf16[128,1024]{1,0:T(8,128)(2,1)S(1)}, bf16[128,1024]{1,0:T(8,128)(2,1)S(1)}, bf16[8,64,896]{2,1,0:T(8,128)(2,1)S(1)}) custom-call(s32[11]{0:T(128)S(1)} %compare_select_fusion.1.ids_ref.refs_1_.refs_0_, bf16[8,64,896]{2,1,0:T(8,128)(2,1)} %bitcast.12, bf16[896,1024]{1,0:T(8,128)(2,1)} %refs_2_.2), custom_call_target="tpu_custom_call" | custom-call | flops 1 | bytes 1 | tf_op jit(solution)/shard_map/pallas_call | solution.py:69
  7.3 1.2 %shard_map.97 = (bf16[128,1024]{1,0:T(8,128)(2,1)S(1)}, bf16[128,1024]{1,0:T(8,128)(2,1)S(1)}) custom-call(s32[11]{0:T(128)S(1)} %compare_select_fusion.1.ids_ref.refs_1_.refs_0_, bf16[8,64,896]{2,1,0:T(8,128)(2,1)S(1)} %get-tuple-element.34.refs_2_.refs_1_, bf16[896,1024]{1,0:T(8,128)(2,1)S(1)} %copy-done), custom_call_target="tpu_custom_call" | custom-call | flops 1 | bytes 1 | tf_op jit(solution)/shard_map/pallas_call | solution.py:37
  9.3 0.8 shard_map.95.refs_0_.refs_1_
  10.9 1.5 %collective-permute-start.5 = (bf16[128,1024]{1,0:T(8,128)(2,1)S(1)}, bf16[128,1024]{1,0:T(8,128)(2,1)S(1)}, u32[]{:S(2)}, u32[]{:S(2)}) collective-permute-start(bf16[128,1024]{1,0:T(8,128)(2,1)S(1)} %shard_map.98.refs_0_.refs_2_), channel_id=1, source_target_pairs={{0,2},{2,0},{1,3},{3,1},{4,6},{6,4},{5,7},{7,5},{8,10},{10,8},{9,1... | collective-permute-start | bytes 786440 | tf_op jit(solution)/shard_map/away1/ppermute | solution.py:262
  14.4 2.1 %shard_map.100 = (bf16[896,1024]{1,0:T(8,128)(2,1)S(1)}, bf16[1024,896]{1,0:T(8,128)(2,1)S(1)}) custom-call(bf16[128,1024]{1,0:T(8,128)(2,1)S(1)} %shard_map.98.refs_0_.refs_2_, bf16[1024,896]{1,0:T(8,128)(2,1)} %collective-permute-done.2.refs_1_), custom_call_target="tpu_custom_call" | custom-call | flops 1 | bytes 1 | tf_op jit(solution)/shard_map/pallas_call | solution.py:37
  18.0 1.1 %collective-permute-start.7 = (bf16[128,896]{1,0:T(8,128)(2,1)S(1)}, bf16[128,896]{1,0:T(8,128)(2,1)S(1)}, u32[]{:S(2)}, u32[]{:S(2)}) collective-permute-start(bf16[128,896]{1,0:T(8,128)(2,1)S(1)} %get-tuple-element.46), channel_id=1, source_target_pairs={{0,24},{8,16},{16,8},{24,0},{1,25},{9,17},{17,9},{25,1},{2,26},{10... | collective-permute-start | bytes 688136 | tf_op jit(solution)/shard_map/g3/ppermute | solution.py:267
  19.4 3.3 %collective-permute-done.5.refs_3_ = bf16[128,1024]{1,0:T(8,128)(2,1)S(1)} collective-permute-done((bf16[128,1024]{1,0:T(8,128)(2,1)S(1)}, bf16[128,1024]{1,0:T(8,128)(2,1)S(1)}, u32[]{:S(2)}, u32[]{:S(2)}) %collective-permute-start.5) | collective-permute-done | bytes 262176 | tf_op jit(solution)/shard_map/away1/ppermute | solution.py:262
  23.7 6.7 %collective-permute-done.7.refs_2_ = bf16[128,896]{1,0:T(8,128)(2,1)S(1)} collective-permute-done((bf16[128,896]{1,0:T(8,128)(2,1)S(1)}, bf16[128,896]{1,0:T(8,128)(2,1)S(1)}, u32[]{:S(2)}, u32[]{:S(2)}) %collective-permute-start.7) | collective-permute-done | bytes 229408 | tf_op jit(solution)/shard_map/g3/ppermute | solution.py:267
  30.5 0.9 %collective-permute-done.8.refs_1_ = bf16[128,896]{1,0:T(8,128)(2,1)S(1)} collective-permute-done((bf16[128,896]{1,0:T(8,128)(2,1)S(1)}, bf16[128,896]{1,0:T(8,128)(2,1)S(1)}, u32[]{:S(2)}, u32[]{:S(2)}) %collective-permute-start.8) | collective-permute-done | bytes 229408 | tf_op jit(solution)/shard_map/g1/ppermute | solution.py:267
  31.4 18.0 %all_to_all.10.refs_1_ = bf16[16,8,896]{2,1,0:T(8,128)(2,1)S(1)} all-to-all(bf16[16,8,896]{2,1,0:T(8,128)(2,1)S(1)} %bitcast.11), channel_id=1, replica_groups=mesh['za'=2,'zb'=2,'zc'=2,'y'=4,'xh'=2,'xl'=2,'c'=2] {'xh','za','zc','zb'}, dimensions={0} | all-to-all | bytes 458752 | tf_op jit(solution)/shard_map/all_to_all | solution.py:332
  50.0 13.3 %all_to_all.11 = bf16[16,8,896]{2,1,0:T(8,128)(2,1)S(1)} all-to-all(bf16[16,8,896]{2,1,0:T(8,128)(2,1)S(1)} %shard_map.108), channel_id=1, replica_groups=mesh['za'=2,'zb'=2,'zc'=2,'y'=4,'xh'=2,'xl'=2,'c'=2] {'xh','za','zc','zb'}, dimensions={0} | all-to-all | bytes 458752 | tf_op jit(solution)/shard_map/all_to_all | solution.py:334
  63.3 1.5 %collective-permute-start.9 = (bf16[128,896]{1,0:T(8,128)(2,1)S(1)}, bf16[128,896]{1,0:T(8,128)(2,1)S(1)}, u32[]{:S(2)}, u32[]{:S(2)}) collective-permute-start(bf16[128,896]{1,0:T(8,128)(2,1)S(1)} %bitcast.5), channel_id=1, source_target_pairs={{0,8},{8,0},{16,24},{24,16},{1,9},{9,1},{17,25},{25,17},{2,10},{10... | collective-permute-start | bytes 688136 | tf_op jit(solution)/shard_map/e1/ppermute | solution.py:267
  64.8 1.9 %collective-permute-start.11 = (bf16[128,896]{1,0:T(8,128)(2,1)S(1)}, bf16[128,896]{1,0:T(8,128)(2,1)S(1)}, u32[]{:S(2)}, u32[]{:S(2)}) collective-permute-start(bf16[128,896]{1,0:T(8,128)(2,1)S(1)} %bitcast.6), channel_id=1, source_target_pairs={{0,24},{8,16},{16,8},{24,0},{1,25},{9,17},{17,9},{25,1},{2,26},{10... | collective-permute-start | bytes 688136 | tf_op jit(solution)/shard_map/e3/ppermute | solution.py:267
  67.4 0.8 collective-permute-done.9.refs_0_.refs_3_.refs_5_
  69.3 1.2 %collective-permute-start.12 = (bf16[64,1024]{1,0:T(8,128)(2,1)S(1)}, bf16[64,1024]{1,0:T(8,128)(2,1)S(1)}, u32[]{:S(2)}, u32[]{:S(2)}) collective-permute-start(bf16[64,1024]{1,0:T(8,128)(2,1)S(1)} %get-tuple-element.49.refs_0_.refs_2_), channel_id=1, source_target_pairs={{0,2},{2,0},{1,3},{3,1},{4,6},{6,4},{5,7},{7,5},{8,10},{10,8},{9,1... | collective-permute-start | bytes 393224 | tf_op jit(solution)/shard_map/back1/ppermute | solution.py:262
  70.5 1.6 %collective-permute-done.11.refs_2_.refs_4_ = bf16[128,896]{1,0:T(8,128)(2,1)S(1)} collective-permute-done((bf16[128,896]{1,0:T(8,128)(2,1)S(1)}, bf16[128,896]{1,0:T(8,128)(2,1)S(1)}, u32[]{:S(2)}, u32[]{:S(2)}) %collective-permute-start.11) | collective-permute-done | bytes 229408 | tf_op jit(solution)/shard_map/e3/ppermute | solution.py:267
  72.1 1.2 %collective-permute-done.10.refs_1_.refs_3_ = bf16[128,896]{1,0:T(8,128)(2,1)S(1)} collective-permute-done((bf16[128,896]{1,0:T(8,128)(2,1)S(1)}, bf16[128,896]{1,0:T(8,128)(2,1)S(1)}, u32[]{:S(2)}, u32[]{:S(2)}) %collective-permute-start.10) | collective-permute-done | bytes 229408 | tf_op jit(solution)/shard_map/e2/ppermute | solution.py:267
  74.7 6.5 %collective-permute-start.14 = (bf16[64,1920]{1,0:T(8,128)(2,1)S(1)}, bf16[64,1920]{1,0:T(8,128)(2,1)S(1)}, u32[]{:S(2)}, u32[]{:S(2)}) collective-permute-start(bf16[64,1920]{1,0:T(8,128)(2,1)S(1)} %get-tuple-element.51), channel_id=1, source_target_pairs={{0,1},{1,0},{2,3},{3,2},{4,5},{5,4},{6,7},{7,6},{8,9},{9,8},{10,11... | collective-permute-start | bytes 737288 | tf_op jit(solution)/shard_map/moved/ppermute | solution.py:262
  81.8 1.1 %collective-permute-start.17 = (bf16[64,1920]{1,0:T(8,128)(2,1)S(1)}, bf16[64,1920]{1,0:T(8,128)(2,1)S(1)}, u32[]{:S(2)}, u32[]{:S(2)}) collective-permute-start(bf16[64,1920]{1,0:T(8,128)(2,1)S(1)} %get-tuple-element.54), channel_id=1, source_target_pairs={{0,1},{1,0},{2,3},{3,2},{4,5},{5,4},{6,7},{7,6},{8,9},{9,8},{10,11... | collective-permute-start | bytes 737288 | tf_op jit(solution)/shard_map/moved/ppermute | solution.py:262
  83.1 0.9 collective-permute-done.17.refs_4_.refs_10_
  84.3 2.5 %collective-permute-start.19 = (bf16[128,1024]{1,0:T(8,128)(2,1)S(1)}, bf16[128,1024]{1,0:T(8,128)(2,1)S(1)}, u32[]{:S(2)}, u32[]{:S(2)}) collective-permute-start(bf16[128,1024]{1,0:T(8,128)(2,1)S(1)} %shard_map.115.refs_0_.refs_2_), channel_id=1, source_target_pairs={{0,1},{1,0},{2,3},{3,2},{4,5},{5,4},{6,7},{7,6},{8,9},{9,8},{10,11... | collective-permute-start | bytes 786440 | tf_op jit(solution)/shard_map/pre0o/ppermute | solution.py:262
  86.9 2.8 %shard_map.116 = (f32[1024,896]{1,0:T(8,128)}, f32[896]{0:T(1024)}, f32[8,128]{1,0:T(8,128)S(1)}) custom-call(bf16[128,1024]{1,0:T(8,128)(2,1)S(1)} %shard_map.115.refs_0_.refs_2_, bf16[1024,256]{1,0:T(8,128)(2,1)S(1)} %shard_map.111.refs_0_.refs_1_, bf16[1024,256]{1,0:T(8,128)(2,1)S(1)} %shard_map.114.refs_0_.refs_2_, ...), custom_call_target="tpu_custom_call" | custom-call | flops 1 | bytes 1 | tf_op jit(solution)/shard_map/pallas_call | solution.py:249
  89.7 2.8 %shard_map.117 = (f32[896,1024]{1,0:T(8,128)}, f32[1024]{0:T(1024)}, f32[8,128]{1,0:T(8,128)}) custom-call(f32[8,128]{1,0:T(8,128)S(1)} %get-tuple-element.55.refs_0_, bf16[896,512]{1,0:T(8,128)(2,1)S(1)} %shard_map.95.refs_0_.refs_1_, bf16[128,1024]{1,0:T(8,128)(2,1)S(1)} %shard_map.115.refs_0_.refs_2_, bf16[128,1024]{1,0:T(8,128)(2,1)S(1)} %shard_map.112.refs_0_.refs_3_, ...), custom_call_target="tpu_custom_call" | custom-call | flops 1 | bytes 1 | tf_op jit(solution)/shard_map/pallas_call | solution.py:249
  (57 shorter events, 11.3 us)
Async XLA Ops:
  0.6 6.7 %copy-start = (bf16[896,1024]{1,0:T(8,128)(2,1)S(1)}, bf16[896,1024]{1,0:T(8,128)(2,1)}, u32[]{:S(2)}) copy-start(bf16[896,1024]{1,0:T(8,128)(2,1)} %refs_2_.2) | copy-start | bytes 5505028
  0.6 13.7 %collective-permute-start.2 = (bf16[1024,896]{1,0:T(8,128)(2,1)}, bf16[1024,896]{1,0:T(8,128)(2,1)}, u32[]{:S(2)}, u32[]{:S(2)}) collective-permute-start(bf16[1024,896]{1,0:T(8,128)(2,1)} %refs_1_.1), channel_id=1, source_target_pairs={{0,1},{1,0},{2,3},{3,2},{4,5},{5,4},{6,7},{7,6},{8,9},{9,8},{10,11... | collective-permute-start | bytes 5505032 | tf_op jit(solution)/shard_map/decoder2/ppermute | solution.py:262
  7.2 1.9 %collective-permute-start = (bf16[128,1024]{1,0:T(8,128)(2,1)S(1)}, bf16[128,1024]{1,0:T(8,128)(2,1)S(1)}, u32[]{:S(2)}, u32[]{:S(2)}) collective-permute-start(bf16[128,1024]{1,0:T(8,128)(2,1)S(1)} %get-tuple-element.33), channel_id=1, source_target_pairs={{0,1},{1,0},{2,3},{3,2},{4,5},{5,4},{6,7},{7,6},{8,9},{9,8},{10,11... | collective-permute-start | bytes 786440 | tf_op jit(solution)/shard_map/got0/ppermute | solution.py:262
  8.6 2.3 %collective-permute-start.1 = (bf16[128,1024]{1,0:T(8,128)(2,1)S(1)}, bf16[128,1024]{1,0:T(8,128)(2,1)S(1)}, u32[]{:S(2)}, u32[]{:S(2)}) collective-permute-start(bf16[128,1024]{1,0:T(8,128)(2,1)S(1)} %get-tuple-element.37), channel_id=1, source_target_pairs={{0,1},{1,0},{2,3},{3,2},{4,5},{5,4},{6,7},{7,6},{8,9},{9,8},{10,11... | collective-permute-start | bytes 786440 | tf_op jit(solution)/shard_map/got1/ppermute | solution.py:262
  9.2 8.0 %collective-permute-start.4 = (bf16[128,1024]{1,0:T(8,128)(2,1)S(1)}, bf16[128,1024]{1,0:T(8,128)(2,1)S(1)}, u32[]{:S(2)}, u32[]{:S(2)}) collective-permute-start(bf16[128,1024]{1,0:T(8,128)(2,1)S(1)} %shard_map.94.refs_0_.refs_4_), channel_id=1, source_target_pairs={{0,2},{2,0},{1,3},{3,1},{4,6},{6,4},{5,7},{7,5},{8,10},{10,8},{9,1... | collective-permute-start | bytes 786440 | tf_op jit(solution)/shard_map/away0/ppermute | solution.py:262
  10.2 3.6 %copy-start.1 = (bf16[1024,896]{1,0:T(8,128)(2,1)S(1)}, bf16[1024,896]{1,0:T(8,128)(2,1)}, u32[]{:S(2)}) copy-start(bf16[1024,896]{1,0:T(8,128)(2,1)} %refs_1_.1) | copy-start | bytes 5505028
  10.9 11.8 %collective-permute-start.5 = (bf16[128,1024]{1,0:T(8,128)(2,1)S(1)}, bf16[128,1024]{1,0:T(8,128)(2,1)S(1)}, u32[]{:S(2)}, u32[]{:S(2)}) collective-permute-start(bf16[128,1024]{1,0:T(8,128)(2,1)S(1)} %shard_map.98.refs_0_.refs_2_), channel_id=1, source_target_pairs={{0,2},{2,0},{1,3},{3,1},{4,6},{6,4},{5,7},{7,5},{8,10},{10,8},{9,1... | collective-permute-start | bytes 786440 | tf_op jit(solution)/shard_map/away1/ppermute | solution.py:262
  13.0 4.1 %copy-start.2 = (f32[1024]{0:T(1024)S(1)}, f32[1024]{0:T(1024)}, u32[]{:S(2)}) copy-start(f32[1024]{0:T(1024)} %refs_4_.1) | copy-start | bytes 12292
  13.1 3.4 %collective-permute-start.3 = (f32[8,896]{1,0:T(8,128)S(1)}, f32[8,896]{1,0:T(8,128)S(1)}, u32[]{:S(2)}, u32[]{:S(2)}) collective-permute-start(f32[8,896]{1,0:T(8,128)S(1)} %get-tuple-element.40), channel_id=1, source_target_pairs={{0,1},{1,0},{2,3},{3,2},{4,5},{5,4},{6,7},{7,6},{8,9},{9,8},{10,11... | collective-permute-start | bytes 86024 | tf_op jit(solution)/shard_map/base2/ppermute | solution.py:262
  18.0 12.4 %collective-permute-start.7 = (bf16[128,896]{1,0:T(8,128)(2,1)S(1)}, bf16[128,896]{1,0:T(8,128)(2,1)S(1)}, u32[]{:S(2)}, u32[]{:S(2)}) collective-permute-start(bf16[128,896]{1,0:T(8,128)(2,1)S(1)} %get-tuple-element.46), channel_id=1, source_target_pairs={{0,24},{8,16},{16,8},{24,0},{1,25},{9,17},{17,9},{25,1},{2,26},{10... | collective-permute-start | bytes 688136 | tf_op jit(solution)/shard_map/g3/ppermute | solution.py:267
  19.1 11.3 %collective-permute-start.6 = (bf16[128,896]{1,0:T(8,128)(2,1)S(1)}, bf16[128,896]{1,0:T(8,128)(2,1)S(1)}, u32[]{:S(2)}, u32[]{:S(2)}) collective-permute-start(bf16[128,896]{1,0:T(8,128)(2,1)S(1)} %get-tuple-element.43.refs_0_), channel_id=1, source_target_pairs={{0,16},{8,24},{16,0},{24,8},{1,17},{9,25},{17,1},{25,9},{2,18},{10... | collective-permute-start | bytes 688136 | tf_op jit(solution)/shard_map/g2/ppermute | solution.py:267
  23.6 7.8 %collective-permute-start.8 = (bf16[128,896]{1,0:T(8,128)(2,1)S(1)}, bf16[128,896]{1,0:T(8,128)(2,1)S(1)}, u32[]{:S(2)}, u32[]{:S(2)}) collective-permute-start(bf16[128,896]{1,0:T(8,128)(2,1)S(1)} %get-tuple-element.47), channel_id=1, source_target_pairs={{0,8},{8,0},{16,24},{24,16},{1,9},{9,1},{17,25},{25,17},{2,10},{10... | collective-permute-start | bytes 688136 | tf_op jit(solution)/shard_map/g1/ppermute | solution.py:267
  63.3 4.9 %collective-permute-start.9 = (bf16[128,896]{1,0:T(8,128)(2,1)S(1)}, bf16[128,896]{1,0:T(8,128)(2,1)S(1)}, u32[]{:S(2)}, u32[]{:S(2)}) collective-permute-start(bf16[128,896]{1,0:T(8,128)(2,1)S(1)} %bitcast.5), channel_id=1, source_target_pairs={{0,8},{8,0},{16,24},{24,16},{1,9},{9,1},{17,25},{25,17},{2,10},{10... | collective-permute-start | bytes 688136 | tf_op jit(solution)/shard_map/e1/ppermute | solution.py:267
  64.8 7.3 %collective-permute-start.11 = (bf16[128,896]{1,0:T(8,128)(2,1)S(1)}, bf16[128,896]{1,0:T(8,128)(2,1)S(1)}, u32[]{:S(2)}, u32[]{:S(2)}) collective-permute-start(bf16[128,896]{1,0:T(8,128)(2,1)S(1)} %bitcast.6), channel_id=1, source_target_pairs={{0,24},{8,16},{16,8},{24,0},{1,25},{9,17},{17,9},{25,1},{2,26},{10... | collective-permute-start | bytes 688136 | tf_op jit(solution)/shard_map/e3/ppermute | solution.py:267
  66.7 6.6 %collective-permute-start.10 = (bf16[128,896]{1,0:T(8,128)(2,1)S(1)}, bf16[128,896]{1,0:T(8,128)(2,1)S(1)}, u32[]{:S(2)}, u32[]{:S(2)}) collective-permute-start(bf16[128,896]{1,0:T(8,128)(2,1)S(1)} %bitcast.7), channel_id=1, source_target_pairs={{0,16},{8,24},{16,0},{24,8},{1,17},{9,25},{17,1},{25,9},{2,18},{10... | collective-permute-start | bytes 688136 | tf_op jit(solution)/shard_map/e2/ppermute | solution.py:267
  68.9 12.4 %collective-permute-start.13 = (bf16[64,1024]{1,0:T(8,128)(2,1)S(1)}, bf16[64,1024]{1,0:T(8,128)(2,1)S(1)}, u32[]{:S(2)}, u32[]{:S(2)}) collective-permute-start(bf16[64,1024]{1,0:T(8,128)(2,1)S(1)} %get-tuple-element.50.refs_3_), channel_id=1, source_target_pairs={{0,2},{2,0},{1,3},{3,1},{4,6},{6,4},{5,7},{7,5},{8,10},{10,8},{9,1... | collective-permute-start | bytes 393224 | tf_op jit(solution)/shard_map/back1/ppermute | solution.py:262
  69.3 12.5 %collective-permute-start.12 = (bf16[64,1024]{1,0:T(8,128)(2,1)S(1)}, bf16[64,1024]{1,0:T(8,128)(2,1)S(1)}, u32[]{:S(2)}, u32[]{:S(2)}) collective-permute-start(bf16[64,1024]{1,0:T(8,128)(2,1)S(1)} %get-tuple-element.49.refs_0_.refs_2_), channel_id=1, source_target_pairs={{0,2},{2,0},{1,3},{3,1},{4,6},{6,4},{5,7},{7,5},{8,10},{10,8},{9,1... | collective-permute-start | bytes 393224 | tf_op jit(solution)/shard_map/back1/ppermute | solution.py:262
  74.0 10.1 %collective-permute-start.18 = (bf16[128,1024]{1,0:T(8,128)(2,1)S(1)}, bf16[128,1024]{1,0:T(8,128)(2,1)S(1)}, u32[]{:S(2)}, u32[]{:S(2)}) collective-permute-start(bf16[128,1024]{1,0:T(8,128)(2,1)S(1)} %shard_map.110.refs_0_.refs_2_), channel_id=1, source_target_pairs={{0,2},{2,0},{1,3},{3,1},{4,6},{6,4},{5,7},{7,5},{8,10},{10,8},{9,1... | collective-permute-start | bytes 786440 | tf_op jit(solution)/shard_map/back0/ppermute | solution.py:262
  74.7 8.2 %collective-permute-start.14 = (bf16[64,1920]{1,0:T(8,128)(2,1)S(1)}, bf16[64,1920]{1,0:T(8,128)(2,1)S(1)}, u32[]{:S(2)}, u32[]{:S(2)}) collective-permute-start(bf16[64,1920]{1,0:T(8,128)(2,1)S(1)} %get-tuple-element.51), channel_id=1, source_target_pairs={{0,1},{1,0},{2,3},{3,2},{4,5},{5,4},{6,7},{7,6},{8,9},{9,8},{10,11... | collective-permute-start | bytes 737288 | tf_op jit(solution)/shard_map/moved/ppermute | solution.py:262
  81.3 1.8 %collective-permute-start.15 = (bf16[64,1920]{1,0:T(8,128)(2,1)S(1)}, bf16[64,1920]{1,0:T(8,128)(2,1)S(1)}, u32[]{:S(2)}, u32[]{:S(2)}) collective-permute-start(bf16[64,1920]{1,0:T(8,128)(2,1)S(1)} %get-tuple-element.52), channel_id=1, source_target_pairs={{0,1},{1,0},{2,3},{3,2},{4,5},{5,4},{6,7},{7,6},{8,9},{9,8},{10,11... | collective-permute-start | bytes 737288 | tf_op jit(solution)/shard_map/moved/ppermute | solution.py:262
  81.4 1.8 %collective-permute-start.16 = (bf16[64,1920]{1,0:T(8,128)(2,1)S(1)}, bf16[64,1920]{1,0:T(8,128)(2,1)S(1)}, u32[]{:S(2)}, u32[]{:S(2)}) collective-permute-start(bf16[64,1920]{1,0:T(8,128)(2,1)S(1)} %get-tuple-element.53), channel_id=1, source_target_pairs={{0,1},{1,0},{2,3},{3,2},{4,5},{5,4},{6,7},{7,6},{8,9},{9,8},{10,11... | collective-permute-start | bytes 737288 | tf_op jit(solution)/shard_map/moved/ppermute | solution.py:262
  81.8 2.2 %collective-permute-start.17 = (bf16[64,1920]{1,0:T(8,128)(2,1)S(1)}, bf16[64,1920]{1,0:T(8,128)(2,1)S(1)}, u32[]{:S(2)}, u32[]{:S(2)}) collective-permute-start(bf16[64,1920]{1,0:T(8,128)(2,1)S(1)} %get-tuple-element.54), channel_id=1, source_target_pairs={{0,1},{1,0},{2,3},{3,2},{4,5},{5,4},{6,7},{7,6},{8,9},{9,8},{10,11... | collective-permute-start | bytes 737288 | tf_op jit(solution)/shard_map/moved/ppermute | solution.py:262
  83.0 6.7 %collective-permute-start.20 = (bf16[128,1024]{1,0:T(8,128)(2,1)S(1)}, bf16[128,1024]{1,0:T(8,128)(2,1)S(1)}, u32[]{:S(2)}, u32[]{:S(2)}) collective-permute-start(bf16[128,1024]{1,0:T(8,128)(2,1)S(1)} %shard_map.112.refs_0_.refs_3_), channel_id=1, source_target_pairs={{0,1},{1,0},{2,3},{3,2},{4,5},{5,4},{6,7},{7,6},{8,9},{9,8},{10,11... | collective-permute-start | bytes 786440 | tf_op jit(solution)/shard_map/pre1o/ppermute | solution.py:262
  84.3 5.4 %collective-permute-start.19 = (bf16[128,1024]{1,0:T(8,128)(2,1)S(1)}, bf16[128,1024]{1,0:T(8,128)(2,1)S(1)}, u32[]{:S(2)}, u32[]{:S(2)}) collective-permute-start(bf16[128,1024]{1,0:T(8,128)(2,1)S(1)} %shard_map.115.refs_0_.refs_2_), channel_id=1, source_target_pairs={{0,1},{1,0},{2,3},{3,2},{4,5},{5,4},{6,7},{7,6},{8,9},{9,8},{10,11... | collective-permute-start | bytes 786440 | tf_op jit(solution)/shard_map/pre0o/ppermute | solution.py:262
  (2 other events, 5.3 us)
